TPU v7x, 256 devices: a whole 4x4x8 slice. The times are simulated.
256 devices in a mesh: lat: 64 (over y, x, z_lo), ch: 4 (over z_hi, core).
Axes of the slice: x: 4, y: 4, z: 8 (z_hi: 2, z_lo: 4; z = z_hi * 4 + z_lo), core: 2. Of those that a mesh axis runs over, the one named last changes fastest.
Arguments:
- fields: bfloat16 [256, 1440, 512], P('lat', None, 'ch'), may hold values from -90 to 90, as said below
- norm_gain: bfloat16 [512], P('ch'), may hold values from 0.099609375 to 1.8984375
- w_qkv: bfloat16 [512, 3, 512], P(None, None, 'ch'), may hold values from -0.25 to 0.25
- w_out: bfloat16 [512, 512], P(None, 'ch'), may hold values from -0.25 to 0.25
- rel_bias: float32 [8, 5, 17], P('ch'), may hold values from -2 to 300
- stencil_reach: int32 [256, 5], P('lat'), may hold values from 0 to 8, as said below
- mode_gain: float32 [96, 512], P(None, 'ch'), may hold values from 0.5 to 5
- w_spec: float32 [512, 512], P(None, 'ch'), may hold values from -0.25 to 0.25
Outputs:
- update: bfloat16 [256, 1440, 512], P('lat', None, 'ch')
Inputs may be any that keep to these rules, and one draw needn't show every extreme that they name: `fields`: activations whose typical size differs between channels and cells. `stencil_reach`: each row offset's half-width is at least 0, the centre offset's at least 1; 8 is reached in every draw.
All inputs are finite; a program needn't handle non-finite values.
Results may differ from a plain program's by a relative error of at most 0.013.
Values may be sent and summed in bfloat16 or wider, within the bound.
A program may use at most 192 MiB of HBM per device.

v0:
```python
import math

import jax
import jax.numpy as jnp
from jax import lax
from jax.sharding import PartitionSpec as P

LON_BLOCK = 160


epsilon = 1e-05
highest = lax.Precision.HIGHEST


def extended_2(cells, sides, width):
    for axis, dim in sides:
        count = lax.axis_size(axis)
        ends = count - 1
        head = lax.slice_in_dim(cells, 0, width, axis=dim)
        tail = lax.slice_in_dim(cells, cells.shape[dim] - width, cells.shape[dim], axis=dim)
        cells = jnp.concatenate(
            [
                lax.ppermute(tail, axis, [(i, (i + 1) % count) for i in range(ends)]),
                cells,
                lax.ppermute(head, axis, [((i + 1) % count, i) for i in range(ends)]),
            ],
            axis=dim,
        )
    return cells


def for_sending(x):

    def short(part):
        return part.astype(jnp.bfloat16) if part.dtype == jnp.float32 else part

    return jax.tree.map(short, x)


def legendre_table(colatitude, degree_count):
    cosine = jnp.cos(colatitude)[:, None]
    log_sine = jnp.log(jnp.sin(colatitude))[:, None]
    orders = jnp.arange(degree_count, dtype=jnp.float32)
    factors = jnp.arange(1, degree_count, dtype=jnp.float32)
    log_ratio = jnp.log((2.0 * factors - 1.0) / (2.0 * factors))
    log_product = jnp.concatenate([jnp.zeros((1,), jnp.float32), jnp.cumsum(log_ratio)])
    diagonal = jnp.exp(
        0.5 * (jnp.log((2.0 * orders + 1.0) / (4.0 * math.pi)) + log_product)[None, :]
        + orders[None, :] * log_sine
    )
    previous = jnp.zeros_like(diagonal)
    earlier = jnp.zeros_like(diagonal)
    levels = []
    for degree in range(degree_count):
        degree_value = float(degree)
        upper_coef = jnp.sqrt(
            max(4.0 * degree_value * degree_value - 1.0, 0.0)
            / jnp.maximum(degree_value * degree_value - orders * orders, 1.0)
        )
        lower_coef = jnp.sqrt(
            jnp.maximum((degree_value - 1.0) ** 2 - orders * orders, 0.0)
            / max(4.0 * (degree_value - 1.0) ** 2 - 1.0, 1.0)
        )
        step_value = upper_coef[None, :] * (cosine * previous - lower_coef[None, :] * earlier)
        current = jnp.where(
            orders[None, :] == degree_value,
            diagonal,
            jnp.where(orders[None, :] < degree_value, step_value, 0.0),
        )
        levels.append(current)
        earlier = previous
        previous = current
    return jnp.stack(levels, axis=1)


def fourier_tables(degree_count, lon_count):
    lon_index = jnp.arange(lon_count, dtype=jnp.int32)
    order_index = jnp.arange(degree_count, dtype=jnp.int32)
    phases = (lon_index[:, None] * order_index[None, :] % lon_count).astype(jnp.float32) * (
        2.0 * math.pi / lon_count
    )
    cosine = jnp.cos(phases)
    sine_table = jnp.sin(phases)
    spacing = 2.0 * math.pi / lon_count
    forward = jnp.stack([cosine, -sine_table], axis=1) * spacing
    factor = jnp.where(order_index == 0, 1.0, 2.0).astype(jnp.float32)[:, None]
    inverse = jnp.stack([cosine.T * factor, -sine_table.T * factor], axis=0)
    return (forward, inverse)


def key_windows(row_block, half_width, lon_block):
    offset_count, lon_count, feature = row_block.shape
    block_count = lon_count // lon_block
    extended = jnp.concatenate(
        [row_block[:, lon_count - half_width :], row_block, row_block[:, : lon_block + half_width]],
        axis=1,
    )
    leading = extended[:, :lon_count].reshape(offset_count, block_count, lon_block, feature)
    trailing = extended[:, lon_block : lon_count + lon_block].reshape(
        offset_count, block_count, lon_block, feature
    )[:, :, : 2 * half_width]
    return jnp.concatenate([leading, trailing], axis=2)


def make_tiles(rel_bias, lon_block):
    half_width = (rel_bias.shape[2] - 1) // 2
    query_pos = jnp.arange(lon_block, dtype=jnp.int32)[:, None]
    key_pos = jnp.arange(lon_block + 2 * half_width, dtype=jnp.int32)[None, :]
    distance = jnp.abs(key_pos - half_width - query_pos)
    onehot = (
        (key_pos - query_pos)[:, :, None]
        == jnp.arange(2 * half_width + 1, dtype=jnp.int32)[None, None, :]
    ).astype(jnp.float32)
    bias_tiles = jnp.einsum("hre,pte->hrpt", rel_bias, onehot, precision=highest)
    return (bias_tiles, distance)


def attend_row(
    query_row,
    key_rows,
    value_rows,
    reach_row,
    valid_rows,
    bias_tiles,
    distance,
    half_width,
    lon_block,
):
    head_count = bias_tiles.shape[0]
    lon_count, feature = query_row.shape
    head_dim = feature // head_count
    block_count = lon_count // lon_block
    key_win = key_windows(key_rows, half_width, lon_block)
    value_win = key_windows(value_rows, half_width, lon_block)
    allowed = (distance[None] <= reach_row[:, None, None]) & valid_rows[:, None, None]
    score_scale = 1.0 / math.sqrt(head_dim)
    pieces = []
    for head_index in range(head_count):
        start_ch = head_index * head_dim
        stop_ch = start_ch + head_dim
        query_head = query_row[:, start_ch:stop_ch].reshape(block_count, lon_block, head_dim)
        scores = (
            jnp.einsum(
                "bpd,rbtd->rbpt",
                query_head,
                key_win[..., start_ch:stop_ch],
                preferred_element_type=jnp.float32,
            )
            * score_scale
            + bias_tiles[head_index][:, None]
        )
        scores = jnp.where(allowed[:, None], scores, -jnp.inf)
        largest = jnp.max(scores, axis=(0, 3), keepdims=True)
        exponent = jnp.exp(scores - largest)
        weights = (exponent / jnp.sum(exponent, axis=(0, 3), keepdims=True)).astype(jnp.bfloat16)
        head_out = jnp.einsum(
            "rbpt,rbtd->bpd",
            weights,
            value_win[..., start_ch:stop_ch],
            preferred_element_type=jnp.float32,
        )
        pieces.append(head_out.reshape(lon_count, head_dim))
    return jnp.concatenate(pieces, axis=1).astype(jnp.bfloat16)


def per_device(fields, norm_gain, w_qkv, w_out, rel_bias, stencil_reach, mode_gain, w_spec):
    row_count, lon_count, local_ch = fields.shape
    channels = w_qkv.shape[0]
    offsets = rel_bias.shape[1]
    radius = offsets // 2
    half_width = rel_bias.shape[2] // 2
    degrees = mode_gain.shape[0]
    lat_count = lax.axis_size("lat")
    lat_total = row_count * lat_count
    first_row = lax.axis_index("lat") * row_count
    weight_flat = w_qkv.reshape(channels, 3 * local_ch)
    fields_float = fields.astype(jnp.float32)
    squares = lax.psum(jnp.sum(fields_float * fields_float, axis=-1, keepdims=True), "ch")
    mean_square = squares / channels
    normed = (
        fields_float * lax.rsqrt(mean_square + epsilon) * norm_gain.astype(jnp.float32)
    ).astype(jnp.bfloat16)
    shard_piece = lax.all_gather(normed, "ch", axis=2, tiled=True)
    weight_rows = weight_flat
    projected = jnp.dot(
        shard_piece.reshape(-1, shard_piece.shape[2]),
        weight_rows,
        preferred_element_type=jnp.float32,
    )
    projected = projected.reshape(row_count, lon_count, 3, local_ch).astype(jnp.bfloat16)
    queries = projected[:, :, 0]
    key_value = projected[:, :, 1:].reshape(row_count, lon_count, 2 * local_ch)
    padded = extended_2(key_value, (("lat", 0),), radius)
    key_padded = padded[..., :local_ch]
    value_padded = padded[..., local_ch:]
    bias_tiles, distance = make_tiles(rel_bias, LON_BLOCK)

    def attend_at(row_index):
        key_rows = lax.dynamic_slice_in_dim(key_padded, row_index, offsets, 0)
        value_rows = lax.dynamic_slice_in_dim(value_padded, row_index, offsets, 0)
        neighbour = first_row + row_index + jnp.arange(offsets, dtype=jnp.int32) - radius
        valid_rows = (neighbour >= 0) & (neighbour < lat_total)
        reach_row = lax.dynamic_index_in_dim(stencil_reach, row_index, 0, keepdims=False)
        query_row = lax.dynamic_index_in_dim(queries, row_index, 0, keepdims=False)
        return attend_row(
            query_row,
            key_rows,
            value_rows,
            reach_row,
            valid_rows,
            bias_tiles,
            distance,
            half_width,
            LON_BLOCK,
        )

    attended = lax.map(attend_at, jnp.arange(row_count, dtype=jnp.int32))
    shard_piece = jax.tree.map(
        lambda part: lax.all_gather(part, "ch", axis=2, tiled=True), for_sending(attended)
    )
    weight_rows = lax.slice_in_dim(w_out, 0, shard_piece.shape[2], axis=0)
    local_part = jnp.zeros((row_count * lon_count, local_ch), jnp.float32) + jnp.dot(
        shard_piece.reshape(-1, shard_piece.shape[2]),
        weight_rows,
        preferred_element_type=jnp.float32,
    )
    mode_count = degrees * degrees
    mode_share = mode_count // lat_count
    forward, inverse = fourier_tables(degrees, lon_count)
    frequency = jnp.einsum("rjc,jsm->rsmc", normed.astype(jnp.float32), forward, precision=highest)
    colatitude = (
        (first_row + jnp.arange(row_count, dtype=jnp.int32)).astype(jnp.float32) + 0.5
    ) * (math.pi / lat_total)
    legendre = legendre_table(colatitude, degrees)
    weighted = legendre * (jnp.sin(colatitude) * (math.pi / lat_total))[:, None, None]
    partial_sums = jnp.einsum("rlm,rsmc->lmsc", weighted, frequency, precision=highest).reshape(
        mode_count, 2, local_ch
    )
    owned_modes = lax.psum_scatter(partial_sums, "lat", scatter_dimension=0, tiled=True)
    mode_start = lax.axis_index("lat") * mode_share
    degree_of = (mode_start + jnp.arange(mode_share, dtype=jnp.int32)) // degrees
    selector = (degree_of[:, None] == jnp.arange(degrees, dtype=jnp.int32)[None, :]).astype(
        jnp.float32
    )
    gain_rows = jnp.dot(selector, mode_gain, precision=highest)
    gained = owned_modes * gain_rows[:, None, :]
    weight_rows = w_spec
    mixed_modes = (
        jnp.zeros((mode_share, 2, local_ch), jnp.float32)
        + jnp.einsum(
            "qsk,ko->qso",
            lax.all_gather(gained.astype(jnp.bfloat16), "ch", axis=2, tiled=True).astype(
                jnp.float32
            ),
            weight_rows,
            precision=highest,
        )
    ).astype(jnp.bfloat16)
    every_mode = lax.all_gather(mixed_modes, "lat", axis=0, tiled=True)
    back_modes = jnp.einsum(
        "rlm,lmsc->rsmc",
        legendre,
        every_mode.reshape(degrees, degrees, 2, local_ch).astype(jnp.float32),
        precision=highest,
    )
    spectral_part = jnp.einsum("rsmc,smj->rjc", back_modes, inverse, precision=highest)
    return (local_part.reshape(row_count, lon_count, local_ch) + spectral_part).astype(jnp.bfloat16)


def solution(mesh):
    in_specs = (
        P("lat", None, "ch"),
        P("ch"),
        P(None, None, "ch"),
        P(None, "ch"),
        P("ch", None, None),
        P("lat", None),
        P(None, "ch"),
        P(None, "ch"),
    )
    out_specs = P("lat", None, "ch")
    return jax.shard_map(
        per_device, mesh=mesh, in_specs=in_specs, out_specs=out_specs, check_vma=False
    )
```

profile of v0, /device:TPU:1, one launch (start us, length us, event | category | flops | bytes accessed | tf_op | source)
XLA Modules:
  0.0 1053.5 jit_solution(15522026073139051903)
XLA Ops:
  9.7 20.8 %psum.7 = f32[4,1440,1]{1,0,2:T(4,128)S(1)} all-reduce(f32[4,1440,1]{1,0,2:T(4,128)S(1)} %bitcast.281), channel_id=1, replica_groups=mesh['lat'=64,'ch'=4] {'ch'}, use_global_device_ids=true, to_apply=%region_1.0 | all-reduce | flops 5760 | bytes 46080 | tf_op jit(solution)/shard_map/psum | solution.py:178
  93.0 13.2 %select_select_fusion = (f32[4,1,96]{1,0,2:T(4,128)}, f32[4,1,96]{1,0,2:T(4,128)}, f32[4,1,96]{1,0,2:T(4,128)}, f32[4,1,96]{1,0,2:T(4,128)}, f32[4,1,96]{1,0,2:T...) fusion(f32[96]{0:T(128)S(1)} %get-tuple-element.615, ...), kind=kLoop, calls=%fused_computation.122 | loop fusion | flops 58368 | bytes 59840 | tf_op jit(solution)/shard_map/jit(_where)/select_n | solution.py:65
  106.2 26.2 %stack.321 = f32[4,96,96]{1,0,2:T(4,128)} concatenate(f32[4,1,96]{1,0,2:T(4,128)} %get-tuple-element.600, f32[4,1,96]{1,0,2:T(4,128)} %get-tuple-element.599, f32[4,1,96]{1,0,2:T(4,128)} %get-tuple-element.598, f32[4,1,96]{1,0,2:T(4,128)} %get-tuple-element.576, f32[4,1,96]{1,0,2:T(4,128)} %get-tuple-element.575, f32[4,1,96]{1,0,2:T(4,128)} %get-tuple-element.574, ...), dimensions={1} | concatenate | bytes 294912 | tf_op jit(solution)/shard_map/stack | solution.py:73
  136.0 7.7 convolution_bitcast_fusion
  143.7 9.2 copy.3205
  154.1 7.8 fusion.39
  164.2 3.7 collective-permute-start
  178.0 32.8 %collective-permute-done = bf16[2,1440,256]{2,1,0:T(8,128)(2,1)} collective-permute-done((bf16[2,1440,256]{2,1,0:T(8,128)(2,1)S(1)}, bf16[2,1440,256]{2,1,0:T(8,128)(2,1)}, u32[]{:S(2)}, u32[]{:S(2)}) %collective-permute-start) | collective-permute-done | bytes 1474592 | tf_op jit(solution)/shard_map/ppermute | solution.py:23
  212.5 67.5 %collective-permute-done.1 = bf16[2,1440,256]{2,1,0:T(8,128)(2,1)S(1)} collective-permute-done((bf16[2,1440,256]{2,1,0:T(8,128)(2,1)S(1)}, bf16[2,1440,256]{2,1,0:T(8,128)(2,1)S(1)}, u32[]{:S(2)}, u32[]{:S(2)}) %collective-permute-start.1) | collective-permute-done | bytes 1474592 | tf_op jit(solution)/shard_map/ppermute | solution.py:25
  283.6 256.9 %reduce-scatter.2.cloned.1.call-done = f32[144,2,128]{2,0,1:T(8,128)} async-done(((f32[9216,2,128]{2,0,1:T(8,128)}), f32[144,2,128]{2,0,1:T(8,128)}) %reduce-scatter.2.cloned.1.call-update) | async-done | bytes 147472 | tf_op jit(solution)/shard_map/reduce_scatter | solution.py:239
  541.4 54.4 %all_gather.14 = bf16[144,2,512]{2,0,1:T(8,128)(2,1)S(1)} all-gather(bf16[144,2,128]{2,0,1:T(8,128)(2,1)S(1)} %multiply_convert_fusion), channel_id=1, replica_groups=mesh['lat'=64,'ch'=4] {'ch'}, dimensions={2}, use_global_device_ids=true | all-gather | bytes 368640 | tf_op jit(solution)/shard_map/all_gather | solution.py:252
  597.0 229.2 %while.13 = (s32[]{:T(128)}, bf16[4,1440,128]{2,1,0:T(8,128)(2,1)}, s32[4]{0:T(128)S(1)}, s32[4,5]{1,0:T(4,128)}, s32[]{:T(128)}, /*index=5*/bf16[8,1440,128]{2,...) while((s32[]{:T(128)}, bf16[4,1440,128]{2,1,0:T(8,128)(2,1)}, ...), condition=%wide.region_7.8_spmd.clone, body=%wide.region_2.7_spmd.clone.sunk | while | flops 710931840 | bytes 127613992 | solution.py:217
  620.6 6.7 fusion.217
  634.9 6.7 fusion.220
  641.9 5.5 fusion.218
  647.4 5.9 fusion.219
  677.7 6.7 fusion.217
  692.1 6.7 fusion.220
  699.0 5.5 fusion.218
  704.6 5.9 fusion.219
  734.9 6.7 fusion.217
  749.3 6.7 fusion.220
  756.2 5.5 fusion.218
  761.8 5.9 fusion.219
  792.1 6.7 fusion.217
  806.4 6.7 fusion.220
  813.4 5.5 fusion.218
  818.9 5.9 fusion.219
  829.6 83.2 %all-gather.8.cloned.1.call-done = bf16[9216,2,128]{2,0,1:T(8,128)(2,1)} async-done(((bf16[144,2,128]{2,0,1:T(8,128)(2,1)}), bf16[9216,2,128]{2,0,1:T(8,128)(2,1)}) %all-gather.8.cloned.1.call-update) | async-done | bytes 4718608 | tf_op jit(solution)/shard_map/all_gather | solution.py:259
  912.8 6.0 fusion.57
  921.6 118.6 %all-gather.6.cloned.1.call-done = bf16[4,1440,512]{2,1,0:T(8,128)(2,1)} async-done(((bf16[4,1440,128]{2,1,0:T(8,128)(2,1)}), bf16[4,1440,512]{2,1,0:T(8,128)(2,1)}) %all-gather.6.cloned.1.call-update) | async-done | bytes 5898256 | tf_op jit(solution)/shard_map/all_gather | solution.py:219
  1040.2 5.5 fusion.44
  (510 shorter events, 210.0 us)
Async XLA Ops:
  7.4 588.5 %copy-start = (f32[512,128]{1,0:T(8,128)S(1)}, f32[512,128]{1,0:T(8,128)}, u32[]{:S(2)}) copy-start(f32[512,128]{1,0:T(8,128)} %param.17) | copy-start | bytes 786436
  7.4 146.8 %all-gather.4.cloned.1.call-start = ((), (), s32[]{:S(2)}) async-start(), calls=%async_computation.1 | async-start | bytes 7372800 | tf_op jit(solution)/shard_map/all_gather | solution.py:183
  34.1 506.4 %reduce-scatter.2.cloned.1.call-start = ((), (), s32[]{:S(2)}) async-start(), calls=%async_computation.3 | async-start | bytes 9584640 | tf_op jit(solution)/shard_map/reduce_scatter | solution.py:239
  106.2 28.7 %copy-start.12 = (bf16[4,1440,128]{2,1,0:T(8,128)(2,1)S(1)}, bf16[4,1440,128]{2,1,0:T(8,128)(2,1)}, u32[]{:S(2)}) copy-start(bf16[4,1440,128]{2,1,0:T(8,128)(2,1)} %fusion.47) | copy-start | bytes 4423684
  152.9 759.8 %all-gather.8.cloned.1.call-start = ((), (), s32[]{:S(2)}) async-start(), calls=%async_computation.4 | async-start | bytes 4792320 | tf_op jit(solution)/shard_map/all_gather | solution.py:259
  164.2 46.5 %collective-permute-start = (bf16[2,1440,256]{2,1,0:T(8,128)(2,1)S(1)}, bf16[2,1440,256]{2,1,0:T(8,128)(2,1)}, u32[]{:S(2)}, u32[]{:S(2)}) collective-permute-start(bf16[2,1440,256]{2,1,0:T(8,128)(2,1)S(1)} %bitcast.279), channel_id=1, source_target_pairs={{0,4},{4,8},{8,12},{12,16},{16,20},{20,24},{24,28},{28,32},{32,36}... | collective-permute-start | bytes 4423688 | tf_op jit(solution)/shard_map/ppermute | solution.py:23
  170.4 41.9 %slice-start = ((s8[4423680]{0:T(1024)(128)(4,1)}), s8[229376]{0:T(1024)(128)(4,1)S(1)}, s32[]{:S(2)}) async-start(s8[4423680]{0:T(1024)(128)(4,1)} %bitcast.276), calls=%async_computation.5 | async-start | bytes 458752
  173.6 38.7 %slice-start.1 = ((s8[4423680]{0:T(1024)(128)(4,1)}), s8[4194304]{0:T(1024)(128)(4,1)S(1)}, s32[]{:S(2)}) async-start(s8[4423680]{0:T(1024)(128)(4,1)} %bitcast.276), calls=%async_computation.6 | async-start | bytes 8388608
  173.8 106.1 %collective-permute-start.1 = (bf16[2,1440,256]{2,1,0:T(8,128)(2,1)S(1)}, bf16[2,1440,256]{2,1,0:T(8,128)(2,1)S(1)}, u32[]{:S(2)}, u32[]{:S(2)}) collective-permute-start(bf16[2,1440,256]{2,1,0:T(8,128)(2,1)S(1)} %bitcast.280), channel_id=1, source_target_pairs={{4,0},{8,4},{12,8},{16,12},{20,16},{24,20},{28,24},{32,28},{36,32}... | collective-permute-start | bytes 4423688 | tf_op jit(solution)/shard_map/ppermute | solution.py:25
  596.9 443.3 %all-gather.6.cloned.1.call-start = ((), (), s32[]{:S(2)}) async-start(), calls=%async_computation.2 | async-start | bytes 7372800 | tf_op jit(solution)/shard_map/all_gather | solution.py:219
  620.6 6.8 copy-start.2
  620.6 6.8 copy-start.3
  629.0 5.9 copy-start.8
  634.9 6.9 copy-start.6
  677.7 6.8 copy-start.2
  677.7 6.8 copy-start.3
  686.2 5.9 copy-start.8
  692.1 6.9 copy-start.6
  699.0 5.6 copy-start.9
  699.0 5.6 copy-start.11
  734.9 6.8 copy-start.2
  734.9 6.8 copy-start.3
  743.3 5.9 copy-start.8
  749.3 6.9 copy-start.6
  756.2 5.6 copy-start.9
  792.0 6.8 copy-start.2
  792.1 6.8 copy-start.3
  800.5 5.9 copy-start.8
  806.4 6.9 copy-start.6
  912.8 6.0 copy-start.14
  912.8 6.0 copy-start.15
  918.8 121.4 %copy-start.18 = (bf16[512,128]{1,0:T(8,128)(2,1)S(1)}, bf16[512,128]{1,0:T(8,128)(2,1)}, u32[]{:S(2)}) copy-start(bf16[512,128]{1,0:T(8,128)(2,1)} %param.13) | copy-start | bytes 393220
  (26 other events, 81.5 us)
Sparse Core Ops, SparseCore 0:
  34.3 89.3 all-gather.3
Sparse Core Ops, SparseCore 1:
  153.0 387.4 reduce-scatter.1
  597.0 315.7 all-gather.7
  914.5 125.6 all-gather.5
where the time goes:
time: 1060 us; the launch traced here: 1050 us
  waiting for transfers between devices  559 us (53%)
  local copies, waits for them, and re-layouts  185 us (17%)
  matrix products  123 us (12%)
  other arithmetic  75.7 us (7%)
  blocking collectives  75.2 us (7%)
  between operations  16.3 us (2%)
  loops' own time  14.4 us (1%)
    reduce_scatter x1, waiting for transfers between devices, per_device(): lax.psum_scatter(partial_sums, 'lat', scatter_dimension=0, tiled=True)  257 us
    all_gather x1, waiting for transfers between devices, per_device(): lax.all_gather(part, 'ch', axis=2, tiled=True)  119 us
    all_gather x1, waiting for transfers between devices, per_device(): every_mode = lax.all_gather(mixed_modes, 'lat', axis=0, tiled=True)  83.2 us
    another operation x71, local copies, waits for them, and re-layouts, legendre_table(): return jnp.stack(levels, axis=1)  77.6 us
    ppermute x1, waiting for transfers between devices, extended_2(): lax.ppermute(head, axis, [((i + 1) % count, i) for i in range(ends)])  67.5 us
    all_gather x1, blocking collectives, per_device(): lax.all_gather(gained.astype(jnp.bfloat16), 'ch', axis=2, tiled=True)  54.4 us
    dot_general x8, matrix products, attend_row(): jnp.einsum('rbpt,rbtd->bpd', weights, value_win[..., start_ch:stop_ch], p...  50.2 us
    dot_general x8, matrix products, attend_row(): jnp.einsum('bpd,rbtd->rbpt', query_head, key_win[..., start_ch:stop_ch],...  37.5 us
  transfers between devices with their start and end apart: 6, of which 5 were waited for; matrix products, arithmetic and copies ran while one was open for 35% of the time, Pallas kernels for 0%

commit v1 on v0

v1 whole, which is shorter than its diff:
```python
import functools
import math

import jax
import jax.numpy as jnp
from jax import lax
from jax.experimental import pallas as pl
from jax.experimental.pallas import tpu as pltpu
from jax.sharding import PartitionSpec as P

MESH = pl.DeviceIdType.MESH
NLON = 1440
NLAT = 256
DEG = 96
LOG2E = 1.4426950408889634
NEG = -1e30
EPS = 1e-05
KB = 48
KEYS = 5 * KB


def win_start(w):
    return (w * 90 // 16) * 16


def ring_dev(w, group):
    return (group * 4 + w // 4, w % 4)


def mult16(v):
    return pl.multiple_of(v, 16)


def place():
    lat = lax.axis_index("lat")
    ch = lax.axis_index("ch")
    return lat, ch, lat // 4, lat % 4


def exchange_kernel(f_ref, m_ref, out_ref, mout_ref, lsem, ssem, rsem, hssem, hrsem, mssem, mrsem):
    lat, ch, group, zlo = place()
    me = zlo * 4 + ch
    bar = pltpu.get_barrier_semaphore()
    has_next = group < 15
    has_prev = group > 0
    for d in range(1, 16):
        w = (me + d) % 16
        pl.semaphore_signal(bar, inc=1, device_id=ring_dev(w, group), device_id_type=MESH)

    @pl.when(has_next)
    def _():
        for k in range(4):
            pl.semaphore_signal(bar, inc=1, device_id=((group + 1) * 4, k), device_id_type=MESH)

    @pl.when(has_prev)
    def _():
        for k in range(4):
            pl.semaphore_signal(bar, inc=1, device_id=((group - 1) * 4 + 3, k), device_id_type=MESH)

    edge = (has_next & (zlo == 3)) | (has_prev & (zlo == 0))
    pl.semaphore_wait(bar, jnp.where(edge, 31, 15))

    def pieces(w):
        s = win_start(w)
        a_src = jnp.where(w == 0, 0, s - 16)
        a_dst = jnp.where(w == 0, 16, 0)
        b_src = jnp.where(w == 0, NLON - 16, jnp.where(w == 15, 0, s + 96))
        b_dst = jnp.where(w == 0, 0, 112)
        return (mult16(a_src), mult16(a_dst), 112), (mult16(b_src), mult16(b_dst), 16)

    row0 = 2 + 4 * zlo

    def send(w, src_row, nrow, dst_row, to_group, ss, rs):
        for src, dst, n in pieces(w):
            pltpu.make_async_remote_copy(
                src_ref=f_ref.at[pl.ds(src_row, nrow), pl.ds(src, n)],
                dst_ref=out_ref.at[pl.ds(dst_row, nrow), ch, pl.ds(dst, n)],
                send_sem=ss,
                recv_sem=rs,
                device_id=ring_dev(w, to_group),
                device_id_type=MESH,
            ).start()

    @pl.when(has_next & (zlo == 3))
    def _():
        def body(d, c):
            send((me + d) % 16, 2, 2, 0, group + 1, hssem.at[0], hrsem.at[0])
            return c

        lax.fori_loop(0, 16, body, 0)

    @pl.when(has_prev & (zlo == 0))
    def _():
        def body(d, c):
            send((me + d) % 16, 0, 2, 18, group - 1, hssem.at[1], hrsem.at[1])
            return c

        lax.fori_loop(0, 16, body, 0)

    def body(d, c):
        w = (me + d) % 16
        pltpu.make_async_remote_copy(
            src_ref=m_ref,
            dst_ref=mout_ref.at[me],
            send_sem=mssem,
            recv_sem=mrsem,
            device_id=ring_dev(w, group),
            device_id_type=MESH,
        ).start()
        send(w, 0, 4, row0, group, ssem, rsem)
        return c

    lax.fori_loop(1, 16, body, 0)
    local = [pltpu.make_async_copy(m_ref, mout_ref.at[me], lsem.at[2])]
    for i, (src, dst, n) in enumerate(pieces(me)):
        local.append(
            pltpu.make_async_copy(
                f_ref.at[:, pl.ds(src, n)], out_ref.at[pl.ds(row0, 4), ch, pl.ds(dst, n)], lsem.at[i]
            )
        )
    for copy in local:
        copy.start()
    for copy in local:
        copy.wait()

    def wait_rows(sem, rows):
        ref = out_ref.at[pl.ds(0, rows // 4)]
        pltpu.make_async_copy(ref, ref, sem).wait()

    wait_rows(ssem, 60)
    wait_rows(rsem, 60)
    meta = mout_ref.at[pl.ds(0, 15)]
    pltpu.make_async_copy(meta, meta, mssem).wait()
    pltpu.make_async_copy(meta, meta, mrsem).wait()

    @pl.when(has_next & (zlo == 3))
    def _():
        wait_rows(hssem.at[0], 32)

    @pl.when(has_prev & (zlo == 0))
    def _():
        wait_rows(hssem.at[1], 32)

    @pl.when(has_prev)
    def _():
        wait_rows(hrsem.at[0], 8)

    @pl.when(has_next)
    def _():
        wait_rows(hrsem.at[1], 8)


def exchange(fields, meta):
    dma = pltpu.SemaphoreType.DMA
    return pl.pallas_call(
        exchange_kernel,
        out_shape=(
            jax.ShapeDtypeStruct((20, 4, 128, 128), jnp.bfloat16),
            jax.ShapeDtypeStruct((16, 8, 128), jnp.float32),
        ),
        in_specs=[pl.BlockSpec(memory_space=pl.ANY)] * 2,
        out_specs=[pl.BlockSpec(memory_space=pl.ANY)] * 2,
        scratch_shapes=[dma((3,)), dma, dma, dma((2,)), dma((2,)), dma, dma],
        compiler_params=pltpu.CompilerParams(collective_id=0, has_side_effects=True),
        name="exchange",
    )(fields, meta)


def back_kernel(y_ref, out_ref, lsem, ssem, rsem):
    lat, ch, group, zlo = place()
    me = zlo * 4 + ch
    bar = pltpu.get_barrier_semaphore()
    for d in range(1, 16):
        w = (me + d) % 16
        pl.semaphore_signal(bar, inc=1, device_id=ring_dev(w, group), device_id_type=MESH)
    pl.semaphore_wait(bar, 15)
    s = mult16(win_start(me))
    wide = win_start(me + 1) - win_start(me) == 96

    def body(d, c):
        w = (me + d) % 16
        for lo, n, cond in ((0, 80, None), (80, 16, wide)):

            def go(lo=lo, n=n):
                pltpu.make_async_remote_copy(
                    src_ref=y_ref.at[pl.ds((w // 4) * 4, 4), w % 4, pl.ds(lo, n)],
                    dst_ref=out_ref.at[:, pl.ds(mult16(s + lo), n)],
                    send_sem=ssem,
                    recv_sem=rsem,
                    device_id=ring_dev(w, group),
                    device_id_type=MESH,
                ).start()

            if cond is None:
                go()
            else:
                pl.when(cond)(go)
        return c

    lax.fori_loop(1, 16, body, 0)

    def local(lo, n):
        copy = pltpu.make_async_copy(
            y_ref.at[pl.ds(zlo * 4, 4), ch, pl.ds(lo, n)], out_ref.at[:, pl.ds(mult16(s + lo), n)], lsem
        )
        copy.start()
        copy.wait()

    local(0, 80)
    pl.when(wide)(lambda: local(80, 16))

    def wait_lons(sem, lons):
        ref = out_ref.at[:, pl.ds(0, lons)]
        pltpu.make_async_copy(ref, ref, sem).wait()

    @pl.when(wide)
    def _():
        wait_lons(ssem, 1440)
        wait_lons(rsem, 1344)

    @pl.when(jnp.logical_not(wide))
    def _():
        wait_lons(ssem, 1200)
        wait_lons(rsem, 1360)


def back(y):
    dma = pltpu.SemaphoreType.DMA
    return pl.pallas_call(
        back_kernel,
        out_shape=jax.ShapeDtypeStruct((4, NLON, 128), jnp.bfloat16),
        in_specs=[pl.BlockSpec(memory_space=pl.ANY)],
        out_specs=pl.BlockSpec(memory_space=pl.ANY),
        scratch_shapes=[dma, dma, dma],
        compiler_params=pltpu.CompilerParams(collective_id=1, has_side_effects=True),
        name="back",
    )(y)


def attend_kernel(x_ref, gain_ref, w_ref, wo_ref, bias_ref, reach_ref, y_ref, q_s, k_s, v_s, b_s, t_s, a_s):
    _, _, group, _ = place()
    lane = lax.broadcasted_iota(jnp.int32, (32, KEYS), 1)
    query = lax.broadcasted_iota(jnp.int32, (32, KEYS), 0)
    offset = sum((lane >= KB * a).astype(jnp.int32) for a in range(1, 5))
    delta = lane - KB * offset - query - 8
    dist = jnp.abs(delta).astype(jnp.float32)
    for h in range(8):
        tile = jnp.full((32, KEYS), NEG, jnp.float32)
        for b in range(17):
            tile = jnp.where(delta == b - 8, bias_ref[h, b : b + 1, :], tile)
        b_s[h // 2, (h % 2) * 32 : (h % 2) * 32 + 32, :] = tile

    def project(step, c):
        rows = pl.ds(step * 4, 4)
        parts = [x_ref[rows, k].reshape(512, 128).astype(jnp.float32) for k in range(4)]
        total = sum(p * p for p in parts)
        square = jnp.sum(total, axis=1, keepdims=True)
        scale = lax.rsqrt(square * (1.0 / 512.0) + EPS)
        outside = ((step == 0) & (group == 0), (step == 4) & (group == 15))
        row = lax.broadcasted_iota(jnp.int32, (512, 1), 0)
        drop = (outside[0] & (row < 256)) | (outside[1] & (row >= 256))
        normed = jnp.concatenate(
            [
                jnp.where(drop, 0.0, p * scale * gain_ref[k : k + 1, :]).astype(jnp.bfloat16)
                for k, p in enumerate(parts)
            ],
            axis=1,
        )
        for t, dst, lo, n, mul in ((0, q_s, 16, 96, LOG2E / 8.0), (1, k_s, 8, 112, None), (2, v_s, 8, 112, None)):
            out = jnp.dot(normed, w_ref[:, t * 512 : t * 512 + 512], preferred_element_type=jnp.float32)
            out = out.reshape(4, 128, 512)[:, lo : lo + n, :]
            if mul is not None:
                out = out * mul
            dst[rows] = out.astype(jnp.bfloat16)
        return c

    lax.fori_loop(0, 5, project, 0)
    left = lax.broadcasted_iota(jnp.int32, (32, 128), 1) < 64

    def attend_row(i, c):
        reach = reach_ref[pl.ds(i, 1), :]
        allowed = dist <= reach
        for hp in range(4):
            t_s[hp, 0:32, :] = jnp.where(allowed, b_s[hp, 0:32, :], NEG)
            t_s[hp, 32:64, :] = jnp.where(allowed, b_s[hp, 32:64, :], NEG)
        for j in range(3):
            for hp in range(4):
                cols = slice(hp * 128, hp * 128 + 128)
                qb = q_s[i + 2, j * 32 : j * 32 + 32, cols]
                zero = jnp.zeros_like(qb)
                qq = jnp.concatenate([jnp.where(left, qb, zero), jnp.where(left, zero, qb)], axis=0)
                kb = k_s[pl.ds(i, 5), j * 32 : j * 32 + KB, cols].reshape(KEYS, 128)
                vb = v_s[pl.ds(i, 5), j * 32 : j * 32 + KB, cols].reshape(KEYS, 128)
                s = lax.dot_general(qq, kb, (((1,), (1,)), ((), ())), preferred_element_type=jnp.float32)
                s = s + t_s[hp]
                top = jnp.max(s, axis=1, keepdims=True)
                p = jnp.exp2(s - top)
                total = jnp.sum(p, axis=1, keepdims=True)
                o = jnp.dot(p.astype(jnp.bfloat16), vb, preferred_element_type=jnp.float32)
                o = o / total
                o = jnp.where(left, o[:32], o[32:])
                a_s[i, j * 32 : j * 32 + 32, cols] = o.astype(jnp.bfloat16)
        return c

    lax.fori_loop(0, 16, attend_row, 0)

    def finish(step, c):
        rows = pl.ds(step * 4, 4)
        att = a_s[rows].reshape(384, 512)
        out = jnp.dot(att, wo_ref[...], preferred_element_type=jnp.float32)
        for k in range(4):
            y_ref[rows, k] = out[:, k * 128 : k * 128 + 128].reshape(4, 96, 128).astype(jnp.bfloat16)
        return c

    lax.fori_loop(0, 4, finish, 0)


def attend(x, gain, w, wo, bias, reach):
    bf = jnp.bfloat16
    vmem = pl.BlockSpec(memory_space=pltpu.VMEM)
    return pl.pallas_call(
        attend_kernel,
        out_shape=jax.ShapeDtypeStruct((16, 4, 96, 128), bf),
        in_specs=[vmem] * 6,
        out_specs=vmem,
        scratch_shapes=[
            pltpu.VMEM((20, 96, 512), bf),
            pltpu.VMEM((20, 112, 512), bf),
            pltpu.VMEM((20, 112, 512), bf),
            pltpu.VMEM((4, 64, KEYS), jnp.float32),
            pltpu.VMEM((4, 64, KEYS), jnp.float32),
            pltpu.VMEM((16, 96, 512), bf),
        ],
        compiler_params=pltpu.CompilerParams(vmem_limit_bytes=48 * 1024 * 1024),
        cost_estimate=pl.CostEstimate(flops=10**10, bytes_accessed=8 * 10**6, transcendentals=0),
        name="attend",
    )(x, gain, w, wo, bias, reach)


def legendre_kernel(m_ref, d_ref, cos_ref, out_ref):
    m = m_ref[...]
    cosine = cos_ref[...]
    diagonal = d_ref[...]

    def step(l, carry):
        previous, earlier = carry
        deg = l.astype(jnp.float32)
        upper = jnp.sqrt(jnp.maximum(4.0 * deg * deg - 1.0, 0.0) / jnp.maximum(deg * deg - m * m, 1.0))
        less = deg - 1.0
        lower = jnp.sqrt(jnp.maximum(less * less - m * m, 0.0) / jnp.maximum(4.0 * less * less - 1.0, 1.0))
        value = upper * (cosine * previous - lower * earlier)
        current = jnp.where(m == deg, diagonal, jnp.where(m < deg, value, 0.0))
        for k in range(3):
            out_ref[k, pl.ds(l, 1), :] = current[k : k + 1, :]
        return current, previous

    zero = diagonal * 0.0
    lax.fori_loop(0, DEG, step, (zero, zero))


def legendre_rows(lat, colatitude):
    pair = lat * 3 + jnp.arange(8, dtype=jnp.int32)
    order = jnp.minimum(pair // 2, DEG - 1)
    factors = jnp.arange(1, DEG, dtype=jnp.float32)
    log_ratio = jnp.log((2.0 * factors - 1.0) / (2.0 * factors))
    log_product = jnp.concatenate([jnp.zeros((1,), jnp.float32), jnp.cumsum(log_ratio)])
    orders = jnp.arange(DEG, dtype=jnp.float32)
    base = 0.5 * (jnp.log((2.0 * orders + 1.0) / (4.0 * math.pi)) + log_product)
    pick = order[:, None] == jnp.arange(DEG, dtype=jnp.int32)[None, :]
    mine = jnp.sum(jnp.where(pick, base[None, :], 0.0), axis=1)
    m = order.astype(jnp.float32)
    diagonal = jnp.exp(mine[:, None] + m[:, None] * jnp.log(jnp.sin(colatitude))[None, :])
    vmem = pl.BlockSpec(memory_space=pltpu.VMEM)
    return pl.pallas_call(
        legendre_kernel,
        out_shape=jax.ShapeDtypeStruct((3, DEG, NLAT), jnp.float32),
        in_specs=[vmem] * 3,
        out_specs=vmem,
        name="legendre",
    )(
        jnp.broadcast_to(m[:, None], (8, NLAT)),
        diagonal,
        jnp.broadcast_to(jnp.cos(colatitude)[None, :], (8, NLAT)),
    )


def wave_table():
    coarse = jnp.arange(45, dtype=jnp.int32) * 32
    fine = jnp.arange(32, dtype=jnp.int32)
    order = jnp.arange(2 * DEG, dtype=jnp.int32) // 2

    def angle(cells):
        return (cells[:, None] * order[None, :] % NLON).astype(jnp.float32) * (2.0 * math.pi / NLON)

    a, b = angle(coarse)[:, None, :], angle(fine)[None, :, :]
    ca, sa, cb, sb = jnp.cos(a), jnp.sin(a), jnp.cos(b), jnp.sin(b)
    even = (jnp.arange(2 * DEG) % 2 == 0)[None, None, :]
    return jnp.where(even, ca * cb - sa * sb, -(sa * cb + ca * sb)).astype(jnp.bfloat16).reshape(NLON, 2 * DEG)


def spectral_modes(fields, norm_gain, mode_gain, w_spec, table):
    bf, f32 = jnp.bfloat16, jnp.float32
    lat = lax.axis_index("lat")
    x = fields.astype(f32)
    squares = lax.psum(jnp.sum(x * x, axis=-1), "ch")
    scale = lax.rsqrt(squares / 512.0 + EPS)
    normed = (x * scale[..., None] * norm_gain.astype(f32)).astype(bf)
    freq = jnp.einsum("rjc,jk->krc", normed, table, preferred_element_type=f32)
    freq = jnp.pad(freq.reshape(64, 12, 128), ((0, 0), (0, 4), (0, 0))).astype(bf)
    got = lax.all_to_all(freq, "lat", 0, 0, tiled=True)[:, :12].reshape(64, 3, 4, 128)
    got = jnp.moveaxis(got, 1, 0).reshape(3, NLAT, 128)
    colatitude = (jnp.arange(NLAT, dtype=jnp.int32).astype(f32) + 0.5) * (math.pi / NLAT)
    legendre = legendre_rows(lat, colatitude)
    weight = jnp.sin(colatitude) * (math.pi / NLAT * 2.0 * math.pi / NLON)
    coef = jnp.einsum("kli,kic->klc", (legendre * weight).astype(bf), got, preferred_element_type=f32)
    gained = (coef * mode_gain[None]).astype(bf).reshape(3 * DEG, 128)
    gained = lax.all_gather(gained, "ch", axis=1, tiled=True)
    mixed = jnp.dot(gained, w_spec.astype(bf), preferred_element_type=f32).astype(bf).reshape(3, DEG, 128)
    modes = jnp.einsum("kli,klc->ikc", legendre.astype(bf), mixed, preferred_element_type=f32)
    factor = jnp.where(lat * 3 + jnp.arange(3) < 2, 1.0, 2.0).astype(f32)
    modes = modes * factor[None, :, None]
    modes = jnp.pad(modes.reshape(64, 12, 128), ((0, 0), (0, 4), (0, 0))).astype(bf)
    modes = lax.all_to_all(modes, "lat", 0, 0, tiled=True)[:, :12].reshape(64, 4, 3, 128)
    return jnp.moveaxis(modes, 1, 0).reshape(4, 2 * DEG, 128)


def per_device(fields, norm_gain, w_qkv, w_out, rel_bias, stencil_reach, mode_gain, w_spec):
    bf, f32 = jnp.bfloat16, jnp.float32
    group = lax.axis_index("lat") // 4
    meta = jnp.concatenate(
        [norm_gain.astype(f32), rel_bias.reshape(170), jnp.zeros((86,), f32), stencil_reach.astype(f32).reshape(20), jnp.zeros((620,), f32)]
    ).reshape(8, 128)
    weights = jnp.concatenate([w_qkv, w_out[:, None, :]], axis=1)
    weights = lax.all_gather(weights, "ch", axis=0, tiled=False)
    x, metas = exchange(fields, meta)
    w_all = jnp.moveaxis(weights, 0, 2)
    w_all = w_all.reshape(512, 2048)
    gain = metas[:4, 0]
    bias = metas[:4, 1:3].reshape(4, 256)[:, :170].reshape(8, 5, 17) * LOG2E
    bias = jnp.repeat(jnp.moveaxis(bias, 1, 2), KB, axis=2)
    reach = metas[::4, 3, :20].reshape(16, 5)
    row = group * 16 + jnp.arange(16, dtype=jnp.int32)[:, None] + jnp.arange(5, dtype=jnp.int32)[None, :] - 2
    reach = jnp.where((row >= 0) & (row < NLAT), reach, -1.0)
    reach = jnp.repeat(reach, KB, axis=1)
    y = attend(x, gain, w_all[:, :1536], w_all[:, 1536:], bias, reach)
    local = back(y)
    table = wave_table()
    modes = spectral_modes(fields, norm_gain, mode_gain, w_spec, table)
    spectral = jnp.einsum("jk,rkc->rjc", table, modes, preferred_element_type=f32)
    return (local.astype(f32) + spectral).astype(bf)


def solution(mesh):
    in_specs = (
        P("lat", None, "ch"),
        P("ch"),
        P(None, None, "ch"),
        P(None, "ch"),
        P("ch", None, None),
        P("lat", None),
        P(None, "ch"),
        P(None, "ch"),
    )
    return jax.shard_map(
        per_device, mesh=mesh, in_specs=in_specs, out_specs=P("lat", None, "ch"), check_vma=False
    )
```

time: 1060 us -> 288 us (0.27)
  waiting for transfers between devices: 559 us -> 9.73 us
  Pallas kernels: 0 us -> 171 us
  local copies, waits for them, and re-layouts: 185 us -> 17.5 us
  matrix products: 123 us -> 5.77 us
  other arithmetic: 75.7 us -> 5.77 us
  blocking collectives: 75.2 us -> 29.9 us
  starting transfers between devices: 5.41 us -> 34.3 us
  loops' own time: 14.4 us -> 0 us
    reduce_scatter x1 -> x0, waiting for transfers between devices: 257 us -> none  [per_device(): lax.psum_scatter(partial_sums, 'lat', scatter_dimension=0, tiled=True)]
    all_gather x3 -> x1, waiting for transfers between devices: 202 us -> 0.02 us  [per_device(): weights = lax.all_gather(weights, 'ch', axis=0, tiled=False)]
    pallas_call x0 -> x4, Pallas kernels: none -> 171 us  [the longest x1 63.9 us: exchange(): pl.pallas_call(exchange_kernel, out_shape=(jax.ShapeDtypeStruct((20, 4, 1...]
    dot_general x25 -> x5, matrix products: 123 us -> 5.77 us  [the longest x1 3.03 us: per_device(): jnp.einsum('jk,rkc->rjc', table, modes, preferred_element_type=f32)]
    ppermute x2 -> x0, waiting for transfers between devices: 100 us -> none  [the longest x1 67.5 us: extended_2(): lax.ppermute(head, axis, [((i + 1) % count, i) for i in range(ends)])]
    another operation x79 -> x2, local copies, waits for them, and re-layouts: 79.7 us -> 0.23 us  [the longest x71 77.6 us: legendre_table(): return jnp.stack(levels, axis=1)]
    all_gather x1, blocking collectives: 54.4 us -> 8.66 us  [spectral_modes(): gained = lax.all_gather(gained, 'ch', axis=1, tiled=True)]
    all_to_all x0 -> x2, starting transfers between devices: none -> 34.3 us  [the longest x1 23.7 us: spectral_modes(): lax.all_to_all(modes, 'lat', 0, 0, tiled=True)[:, :12]]
  transfers between devices with their start and end apart: 6 -> 3, of which waited for: 5 -> 1; matrix products, arithmetic and copies ran while one was open for 35% -> 5% of each run, Pallas kernels for 0% -> 24%
where the time goes in v1:
time: 288 us; the launch traced here: 287 us
  Pallas kernels  171 us (59%)
  starting transfers between devices  34.3 us (12%)
  blocking collectives  29.9 us (10%)
  local copies, waits for them, and re-layouts  17.5 us (6%)
  between operations  13.9 us (5%)
  waiting for transfers between devices  9.73 us (3%)
  other arithmetic  5.77 us (2%)
  matrix products  5.77 us (2%)
    pallas_call x1, Pallas kernels, exchange(): pl.pallas_call(exchange_kernel, out_shape=(jax.ShapeDtypeStruct((20, 4, 1...  63.9 us
    pallas_call x1, Pallas kernels, attend(): pl.pallas_call(attend_kernel, out_shape=jax.ShapeDtypeStruct((16, 4, 96,...  62.1 us
    pallas_call x1, Pallas kernels, back(): pl.pallas_call(back_kernel, out_shape=jax.ShapeDtypeStruct((4, NLON, 128)...  40.2 us
    all_to_all x1, starting transfers between devices, spectral_modes(): lax.all_to_all(modes, 'lat', 0, 0, tiled=True)[:, :12]  23.7 us
    psum x1, blocking collectives, spectral_modes(): squares = lax.psum(jnp.sum(x * x, axis=-1), 'ch')  21.2 us
    all_to_all x1, starting transfers between devices, spectral_modes(): lax.all_to_all(freq, 'lat', 0, 0, tiled=True)[:, :12].reshape(64, 3, 4, 128)  10.6 us
    all_to_all x1, waiting for transfers between devices, spectral_modes(): lax.all_to_all(modes, 'lat', 0, 0, tiled=True)[:, :12]  9.69 us
    all_gather x1, blocking collectives, spectral_modes(): gained = lax.all_gather(gained, 'ch', axis=1, tiled=True)  8.66 us
  transfers between devices with their start and end apart: 3, of which 1 were waited for; matrix products, arithmetic and copies ran while one was open for 5% of the time, Pallas kernels for 24%

profile of v1, /device:TPU:1, one launch (start us, length us, event | category | flops | bytes accessed | tf_op | source)
XLA Modules:
  0.0 287.5 jit_solution(11546804358177558382)
XLA Ops:
  6.5 1.9 pad_maximum_fusion
  8.7 0.3 fusion.28
  9.0 0.6 add_negate_fusion
  9.6 0.3 copy.45
  9.9 0.3 copy.46
  10.2 0.8 copy-done.1
  10.9 0.9 fusion.2
  11.9 21.2 %psum.7 = f32[4,1440]{1,0:T(4,128)S(1)} all-reduce(f32[4,1440]{1,0:T(4,128)S(1)} %fusion.2), channel_id=1, replica_groups=mesh['lat'=64,'ch'=4] {'ch'}, use_global_device_ids=true, to_apply=%region_3.4 | all-reduce | flops 5760 | bytes 46080 | tf_op jit(solution)/shard_map/psum | solution.py:405
  33.1 1.1 fusion.10
  34.5 0.8 pad.9
  35.2 10.6 %all-to-all-start = ((bf16[64,16,128]{2,1,0:T(8,128)(2,1)}), bf16[64,16,128]{2,1,0:T(8,128)(2,1)S(1)}, u32[]{:S(2)}, u32[]{:S(2)}) async-start(bf16[64,16,128]{2,1,0:T(8,128)(2,1)} %pad.9), calls=%async_computation | async-start | bytes 524288 | tf_op jit(solution)/shard_map/all_to_all | solution.py:410
  46.1 0.7 concatenate.13
  46.8 63.9 %exchange.1 = (bf16[20,4,128,128]{3,2,1,0:T(8,128)(2,1)}, f32[16,8,128]{2,1,0:T(8,128)}) custom-call(bf16[4,1440,128]{2,1,0:T(8,128)(2,1)} %f_ref.1, f32[8,128]{1,0:T(8,128)} %bitcast.63), custom_call_target="tpu_custom_call" | custom-call | tf_op jit(solution)/shard_map/exchange/pallas_call | solution.py:155
  110.7 0.8 slice_reduce_fusion
  111.6 0.7 slice_bitcast_fusion
  113.0 0.7 add_exponential_fusion.d_ref
  113.7 0.7 broadcast_in_dim.87.m_ref
  114.3 0.6 broadcast_in_dim.90.cos_ref
  114.9 4.4 %legendre.1 = f32[3,96,256]{2,1,0:T(8,128)} custom-call(f32[8,256]{1,0:T(8,128)} %broadcast_in_dim.87.m_ref, f32[8,256]{1,0:T(8,128)} %add_exponential_fusion.d_ref, f32[8,256]{1,0:T(8,128)} %broadcast_in_dim.90.cos_ref), custom_call_target="tpu_custom_call" | custom-call | tf_op jit(solution)/shard_map/legendre/pallas_call | solution.py:374
  119.7 1.2 fusion.14
  120.8 8.7 %all_gather.11 = bf16[288,512]{1,0:T(8,128)(2,1)S(1)} all-gather(bf16[288,128]{1,0:T(8,128)(2,1)S(1)} %bitcast.60), channel_id=1, replica_groups=mesh['lat'=64,'ch'=4] {'ch'}, dimensions={1}, use_global_device_ids=true | all-gather | bytes 368640 | tf_op jit(solution)/shard_map/all_gather | solution.py:417
  129.8 0.3 fusion.13
  130.4 0.8 pad.10
  131.2 23.7 %all-to-all-start.1 = ((bf16[64,16,128]{2,1,0:T(8,128)(2,1)}), bf16[64,16,128]{2,1,0:T(8,128)(2,1)S(1)}, u32[]{:S(2)}, u32[]{:S(2)}) async-start(bf16[64,16,128]{2,1,0:T(8,128)(2,1)} %pad.10), calls=%async_computation.1 | async-start | bytes 524288 | tf_op jit(solution)/shard_map/all_to_all | solution.py:423
  155.8 0.5 select_convert_fusion
  156.2 9.7 %all-to-all-done.1 = bf16[64,16,128]{2,1,0:T(8,128)(2,1)S(1)} async-done(((bf16[64,16,128]{2,1,0:T(8,128)(2,1)}), bf16[64,16,128]{2,1,0:T(8,128)(2,1)S(1)}, u32[]{:S(2)}, u32[]{:S(2)}) %all-to-all-start.1) | async-done | bytes 262176 | tf_op jit(solution)/shard_map/all_to_all | solution.py:423
  166.1 4.6 %copy.62 = bf16[4,512,4,128]{3,0,2,1:T(4,128)(2,1)} copy(bf16[4,512,4,128]{3,1,0,2:T(8,128)(2,1)} %bitcast.52) | data formatting | bytes 4194304 | tf_op jit(solution)/shard_map/all_gather | solution.py:434
  170.7 3.3 %reshape.368 = bf16[512,2048]{1,0:T(8,128)(2,1)S(1)} reshape(bf16[512,4,4,128]{3,2,1,0:T(4,128)(2,1)} %bitcast.48) | data formatting | bytes 4194304 | tf_op jit(solution)/shard_map/reshape | solution.py:437
  174.2 62.1 %attend.1.y_ref = bf16[16,4,96,128]{3,2,1,0:T(8,128)(2,1)S(1)} custom-call(bf16[20,4,128,128]{3,2,1,0:T(8,128)(2,1)} %get-tuple-element.7.x_ref, f32[4,128]{1,0:T(4,128)S(1)} %slice_bitcast_fusion.1.gain_ref, bf16[512,1536]{1,0:T(8,128)(2,1)S(1)} %slice.33.w_ref, bf16[512,512]{1,0:T(8,128)(2,1)S(1)} %slice.34.wo_ref, f32[8,17,240]{2,1,0:T(8,128)S(1)} %copy.44.bias_ref, ...), custom_call_target="tpu_custom_call" | custom-call | flops 10000000000 | bytes 8000000 | tf_op jit(solution)/shard_map/attend/pallas_call | solution.py:321
  236.3 1.1 copy-done
  237.4 40.2 %back.1 = bf16[4,1440,128]{2,1,0:T(8,128)(2,1)} custom-call(bf16[16,4,96,128]{3,2,1,0:T(8,128)(2,1)} %copy-done), custom_call_target="tpu_custom_call" | custom-call | tf_op jit(solution)/shard_map/back/pallas_call | solution.py:229
  277.6 3.0 %fusion.1 = bf16[4,1440,128]{2,1,0:T(8,128)(2,1)} fusion(bf16[1440,192,1]{1,0,2:T(8,128)(2,1)S(1)} %bitcast.51, bf16[4,1440,128]{2,1,0:T(8,128)(2,1)} %back.1, bf16[4,192,128]{2,0,1:T(4,128)(2,1)S(1)} %bitcast.58), kind=kOutput, calls=%fused_computation.4 | convolution fusion | flops 285327360 | bytes 3698688 | tf_op jit(solution)/shard_map/jk,rkc->rjc/dot_general | solution.py:449
  (83 shorter events, 3.5 us)
Async XLA Ops:
  6.5 159.6 %all-gather.3.cloned.1.call-start = ((), (), s32[]{:S(2)}) async-start(), calls=%async_computation.2 | async-start | bytes 2621440 | tf_op jit(solution)/shard_map/all_gather | solution.py:434
  8.7 0.9 copy-start.7
  8.7 0.9 copy-start.9
  9.0 0.6 copy-start.3
  9.0 0.6 copy-start.5
  9.6 1.4 copy-start.1
  9.9 23.2 %copy-start.16 = (bf16[128]{0:T(256)(128)(2,1)S(1)}, bf16[128]{0:T(256)(128)(2,1)}, u32[]{:S(2)}) copy-start(bf16[128]{0:T(256)(128)(2,1)} %param.9) | copy-start | bytes 772
  34.2 11.7 %copy-start.14 = (f32[2,5,17]{2,0,1:T(2,128)S(1)}, f32[2,5,17]{2,0,1:T(2,128)}, u32[]{:S(2)}) copy-start(f32[2,5,17]{2,0,1:T(2,128)} %param.12) | copy-start | bytes 2044
  34.2 11.7 %copy-start.15 = (s32[4,5]{1,0:T(4,128)S(1)}, s32[4,5]{1,0:T(4,128)}, u32[]{:S(2)}) copy-start(s32[4,5]{1,0:T(4,128)} %param.13) | copy-start | bytes 244
  35.2 84.2 %all-to-all-start = ((bf16[64,16,128]{2,1,0:T(8,128)(2,1)}), bf16[64,16,128]{2,1,0:T(8,128)(2,1)S(1)}, u32[]{:S(2)}, u32[]{:S(2)}) async-start(bf16[64,16,128]{2,1,0:T(8,128)(2,1)} %pad.9), calls=%async_computation | async-start | bytes 524288 | tf_op jit(solution)/shard_map/all_to_all | solution.py:410
  46.8 72.9 %copy-start.13 = (f32[96,128]{1,0:T(8,128)S(1)}, f32[96,128]{1,0:T(8,128)}, u32[]{:S(2)}) copy-start(f32[96,128]{1,0:T(8,128)} %param.14) | copy-start | bytes 147460
  110.7 18.8 %copy-start.11 = (f32[512,128]{1,0:T(8,128)S(1)}, f32[512,128]{1,0:T(8,128)}, u32[]{:S(2)}) copy-start(f32[512,128]{1,0:T(8,128)} %param.15) | copy-start | bytes 786436
  119.3 10.4 %copy-start.2 = (f32[3,96,256]{2,1,0:T(8,128)S(1)}, f32[3,96,256]{2,1,0:T(8,128)}, u32[]{:S(2)}) copy-start(f32[3,96,256]{2,1,0:T(8,128)} %legendre.1) | copy-start | bytes 884740
  129.5 25.4 %copy-start.12 = (f32[16,8,128]{2,1,0:T(8,128)S(1)}, f32[16,8,128]{2,1,0:T(8,128)}, u32[]{:S(2)}) copy-start(f32[16,8,128]{2,1,0:T(8,128)} %get-tuple-element.8) | copy-start | bytes 196612
  130.4 25.3 %copy-start.4 = (f32[45,192]{1,0:T(8,128)S(1)}, f32[45,192]{1,0:T(8,128)}, u32[]{:S(2)}) copy-start(f32[45,192]{1,0:T(8,128)} %copy-done.3) | copy-start | bytes 103684
  130.4 25.3 %copy-start.6 = (f32[45,192]{1,0:T(8,128)S(1)}, f32[45,192]{1,0:T(8,128)}, u32[]{:S(2)}) copy-start(f32[45,192]{1,0:T(8,128)} %copy-done.5) | copy-start | bytes 103684
  130.4 25.3 %copy-start.8 = (f32[32,192]{1,0:T(8,128)S(1)}, f32[32,192]{1,0:T(8,128)}, u32[]{:S(2)}) copy-start(f32[32,192]{1,0:T(8,128)} %copy-done.7) | copy-start | bytes 73732
  130.4 25.3 %copy-start.10 = (f32[32,192]{1,0:T(8,128)S(1)}, f32[32,192]{1,0:T(8,128)}, u32[]{:S(2)}) copy-start(f32[32,192]{1,0:T(8,128)} %copy-done.9) | copy-start | bytes 73732
  131.2 34.7 %all-to-all-start.1 = ((bf16[64,16,128]{2,1,0:T(8,128)(2,1)}), bf16[64,16,128]{2,1,0:T(8,128)(2,1)S(1)}, u32[]{:S(2)}, u32[]{:S(2)}) async-start(bf16[64,16,128]{2,1,0:T(8,128)(2,1)} %pad.10), calls=%async_computation.1 | async-start | bytes 524288 | tf_op jit(solution)/shard_map/all_to_all | solution.py:423
  236.3 1.2 copy-start
Sparse Core Ops, SparseCore 0:
  9.2 45.0 all-gather.2

commit v2 on v0

v2 whole, which is shorter than its diff:
```python
import math

import jax
import jax.numpy as jnp
from jax import lax
from jax.experimental import pallas as pl
from jax.experimental.pallas import tpu as pltpu
from jax.sharding import PartitionSpec as P

MESH = pl.DeviceIdType.MESH
NLON = 1440
NLAT = 256
DEG = 96
OCT = 180
LOG2E = 1.4426950408889634
NEG = -1e30
EPS = 1e-05
KB = 48
KEYS = 5 * KB
F32 = jnp.float32
BF = jnp.bfloat16
DMA = pltpu.SemaphoreType.DMA
VMEM = pl.BlockSpec(memory_space=pltpu.VMEM)
ANY = pl.BlockSpec(memory_space=pl.ANY)
TN = (((0,), (0,)), ((), ()))
NT = (((1,), (1,)), ((), ()))


def win_start(w):
    return 45 * w // 4


def ring_dev(w, group):
    return (group * 4 + w // 4, w % 4)


def place():
    lat = lax.axis_index("lat")
    ch = lax.axis_index("ch")
    return lat, ch, lat // 4, lat % 4


def signal(device):
    pl.semaphore_signal(pltpu.get_barrier_semaphore(), inc=1, device_id=device, device_id_type=MESH)


def remote(src, dst, ss, rs, device):
    pltpu.make_async_remote_copy(
        src_ref=src, dst_ref=dst, send_sem=ss, recv_sem=rs, device_id=device, device_id_type=MESH
    ).start()


def wait_bytes(ref, sem):
    pltpu.make_async_copy(ref, ref, sem).wait()


def loop(lo, hi, body):
    def step(i, c):
        body(i)
        return c

    lax.fori_loop(lo, hi, step, 0)


def sort_rows():
    n = lax.broadcasted_iota(jnp.int32, (1024, 1), 0)
    slot = n % 16
    source = jnp.where(slot < 12, (slot % 4) * 192 + (slot // 4) * 64 + n // 16, -1)
    return (lax.broadcasted_iota(jnp.int32, (1024, 768), 1) == source).astype(F32).astype(BF)


def gather_kernel(
    f_ref, sq_ref, meta_ref, gw_ref, ca_ref, sa_ref, u_ref, v_ref, m_ref, diag_ref, cos_ref,
    win_ref, metas_ref, modes_ref, e_ref, t_ref,
    x_s, stat_s, tab_s, leg_s, send_s,
    lsem, ssem, rsem, hssem, hrsem, mssem, mrsem, qssem, qrsem, assem, arsem,
):
    lat, ch, group, zlo = place()
    me = zlo * 4 + ch
    has_next = group < 15
    has_prev = group > 0
    up = has_next & (zlo == 3)
    down = has_prev & (zlo == 0)
    loop(1, 64, lambda d: signal(((lat + d) % 64, ch)))
    loop(1, 16, lambda d: signal(ring_dev((me + d) % 16, group)))

    @pl.when(has_next)
    def _():
        for k in range(4):
            signal(((group + 1) * 4, k))

    @pl.when(has_prev)
    def _():
        for k in range(4):
            signal(((group - 1) * 4 + 3, k))

    def interleave(c):
        lon = pl.ds(pl.multiple_of(c * 144, 16), 144)
        for a in range(2):
            two = [f_ref[2 * a + b, lon, :].astype(F32).reshape(18, 8, 128) for b in range(2)]
            x_s[a, pl.ds(c * 18, 18)] = jnp.stack(two, axis=1).reshape(18, 16, 128).astype(BF)

    loop(0, 10, interleave)
    stat_s[ch] = sq_ref[...]
    pl.semaphore_wait(pltpu.get_barrier_semaphore(), jnp.where(up | down, 94, 78))

    for d in range(1, 4):
        remote(sq_ref, stat_s.at[ch], qssem, qrsem, (lat, (ch + d) % 4))
    for d in range(1, 4):
        remote(meta_ref, metas_ref.at[me], mssem, mrsem, (lat, (ch + d) % 4))
        remote(meta_ref, metas_ref.at[me], mssem, mrsem, (group * 4 + (zlo + d) % 4, ch))
    mcopy = pltpu.make_async_copy(meta_ref, metas_ref.at[me], lsem.at[2])
    mcopy.start()

    def move(w, src_pair, pairs, dst_pair, to_group, start):
        s = win_start(w)
        src, dst = pl.ds(src_pair, pairs), pl.ds(dst_pair, pairs)
        edge = (w == 0) | (w == 15)

        @pl.when(edge)
        def _():
            a_src = jnp.where(w == 0, 0, s - 1)
            a_dst = jnp.where(w == 0, 1, 0)
            b_src = jnp.where(w == 0, OCT - 1, 0)
            b_dst = jnp.where(w == 0, 0, 13)
            start(x_s.at[src, pl.ds(a_src, 13)], win_ref.at[dst, ch, pl.ds(a_dst, 13)], 0)
            start(x_s.at[src, pl.ds(b_src, 1)], win_ref.at[dst, ch, pl.ds(b_dst, 1)], 1)

        @pl.when(jnp.logical_not(edge))
        def _():
            start(x_s.at[src, pl.ds(s - 1, 14)], win_ref.at[dst, ch], 0)

    def send(w, src_pair, pairs, dst_pair, to_group, ss, rs):
        move(w, src_pair, pairs, dst_pair, to_group,
             lambda a, b, n: remote(a, b, ss, rs, ring_dev(w, to_group)))

    @pl.when(up)
    def _():
        loop(0, 16, lambda d: send((me + d) % 16, 1, 1, 0, group + 1, hssem.at[0], hrsem.at[0]))

    @pl.when(down)
    def _():
        loop(0, 16, lambda d: send((me + d) % 16, 0, 1, 9, group - 1, hssem.at[1], hrsem.at[1]))

    pair0 = 1 + 2 * zlo
    loop(1, 16, lambda d: send((me + d) % 16, 0, 2, pair0, group, ssem, rsem))
    move(me, 0, 2, pair0, group, lambda a, b, n: pltpu.make_async_copy(a, b, lsem.at[n]).start())

    for a in range(12):
        n = min(128, NLON - a * 128)
        tab = ca_ref[:, a : a + 1] * u_ref[...] + sa_ref[:, a : a + 1] * v_ref[...]
        tab_s[:, a * 128 : a * 128 + n] = tab[:, :n]
        t_ref[:, a * 128 : a * 128 + n] = tab[:, :n].astype(BF)

    m = m_ref[...]
    cosine = cos_ref[...]
    diagonal = diag_ref[...]

    def degree(l, carry):
        previous, earlier = carry
        deg = l.astype(F32)
        less = deg - 1.0
        upper = jnp.sqrt(jnp.maximum(4.0 * deg * deg - 1.0, 0.0) / jnp.maximum(deg * deg - m * m, 1.0))
        lower = jnp.sqrt(jnp.maximum(less * less - m * m, 0.0) / jnp.maximum(4.0 * less * less - 1.0, 1.0))
        value = upper * (cosine * previous - lower * earlier)
        current = jnp.where(m == deg, diagonal, jnp.where(m < deg, value, 0.0))
        leg_s[l] = current
        return current, previous

    zero = diagonal * 0.0

    wait_bytes(stat_s.at[pl.ds(0, 3)], qrsem)
    scale = lax.rsqrt((stat_s[0] + stat_s[1] + stat_s[2] + stat_s[3]) * (1.0 / 512.0) + EPS)
    freq = []
    for r in range(4):
        lhs = (tab_s[...] * scale[r : r + 1, :]).astype(BF)
        out = jnp.dot(lhs, f_ref[r], preferred_element_type=F32)
        freq.append((out * gw_ref[r : r + 1, :]).astype(BF))
    out = jnp.dot(sort_rows(), jnp.concatenate(freq, axis=0), preferred_element_type=F32)
    send_s[...] = out.astype(BF).reshape(64, 16, 128)
    loop(1, 64, lambda d: remote(send_s.at[(lat + d) % 64], modes_ref.at[lat], assem, arsem, ((lat + d) % 64, ch)))
    acopy = pltpu.make_async_copy(send_s.at[lat], modes_ref.at[lat], lsem.at[3])
    acopy.start()

    lax.fori_loop(0, DEG, degree, (zero, zero))
    kind = (lax.broadcasted_iota(jnp.int32, (DEG, 128), 1) % 16) // 4
    for c in range(8):
        part = leg_s[:, c, :]
        for k in range(3):
            e_ref[k * DEG : k * DEG + DEG, c * 128 : c * 128 + 128] = jnp.where(kind == k, part, 0.0).astype(BF)

    mcopy.wait()
    acopy.wait()
    pair = win_ref.at[pl.ds(pair0, 2), ch]

    @pl.when((me == 0) | (me == 15))
    def _():
        wait_bytes(win_ref.at[pl.ds(pair0, 2), ch, pl.ds(0, 13)], lsem.at[0])
        wait_bytes(win_ref.at[pl.ds(pair0, 2), ch, pl.ds(0, 1)], lsem.at[1])

    @pl.when((me != 0) & (me != 15))
    def _():
        wait_bytes(pair, lsem.at[0])

    wait_bytes(stat_s.at[pl.ds(0, 3)], qssem)
    wait_bytes(metas_ref.at[pl.ds(0, 6)], mssem)
    wait_bytes(metas_ref.at[pl.ds(0, 6)], mrsem)
    wait_bytes(modes_ref.at[pl.ds(0, 63)], assem)
    wait_bytes(modes_ref.at[pl.ds(0, 63)], arsem)
    most = win_ref.at[:, pl.ds(0, 3)]
    wait_bytes(most, ssem)
    wait_bytes(most, rsem)
    pl.when(up)(lambda: wait_bytes(win_ref.at[pl.ds(0, 4)], hssem.at[0]))
    pl.when(down)(lambda: wait_bytes(win_ref.at[pl.ds(0, 4)], hssem.at[1]))
    pl.when(has_prev)(lambda: wait_bytes(win_ref.at[0], hrsem.at[0]))
    pl.when(has_next)(lambda: wait_bytes(win_ref.at[0], hrsem.at[1]))


def gather(*args):
    shape = jax.ShapeDtypeStruct
    return pl.pallas_call(
        gather_kernel,
        out_shape=(
            shape((10, 4, 14, 16, 128), BF),
            shape((16, 24, 128), F32),
            shape((64, 16, 128), BF),
            shape((3 * DEG, 1024), BF),
            shape((2 * DEG, NLON), BF),
        ),
        in_specs=[VMEM] * 11,
        out_specs=[ANY, ANY, ANY, VMEM, VMEM],
        scratch_shapes=[
            pltpu.VMEM((2, OCT, 16, 128), BF),
            pltpu.VMEM((4, 4, NLON), F32),
            pltpu.VMEM((2 * DEG, NLON), F32),
            pltpu.VMEM((DEG, 8, 128), F32),
            pltpu.VMEM((64, 16, 128), BF),
            DMA((4,)), DMA, DMA, DMA((2,)), DMA((2,)), DMA, DMA, DMA, DMA, DMA, DMA,
        ],
        compiler_params=pltpu.CompilerParams(
            collective_id=0, has_side_effects=True, vmem_limit_bytes=40 * 1024 * 1024
        ),
        name="gather",
    )(*args)


def attend_kernel(
    x_ref, metas_ref, w_ref, got_ref, e_ref, mg_ref, ws_ref,
    out_ref, modes_ref,
    q_s, k_s, v_s, b_s, t_s, a_s, s_s, p_s, l_s, r_s, w_s, y_s, g_s, send_s,
    lsem, ssem, rsem, gssem, grsem, assem, arsem,
):
    lat, ch, group, zlo = place()
    me = zlo * 4 + ch
    loop(1, 64, lambda d: signal(((lat + d) % 64, ch)))
    loop(1, 16, lambda d: signal(ring_dev((me + d) % 16, group)))

    coef = jnp.dot(e_ref[...], got_ref[...].reshape(1024, 128), preferred_element_type=F32)
    coef = coef.reshape(3, DEG, 128) * mg_ref[...][None]
    g_s[ch] = coef.reshape(3 * DEG, 128).astype(BF)
    pl.semaphore_wait(pltpu.get_barrier_semaphore(), 78)
    for d in range(1, 4):
        remote(g_s.at[ch], g_s.at[ch], gssem, grsem, (lat, (ch + d) % 4))

    for t in range(4):
        for k in range(4):
            w_s[t, :, k * 128 : k * 128 + 128] = w_ref[k, t]

    lane = lax.broadcasted_iota(jnp.int32, (32, KEYS), 1)
    query = lax.broadcasted_iota(jnp.int32, (32, KEYS), 0)
    row_of = sum((lane >= KB * a).astype(jnp.int32) for a in range(1, 5))
    delta = lane - KB * row_of - query - 8
    dist = jnp.abs(delta).astype(F32)
    lane8 = lax.broadcasted_iota(jnp.int32, (8, KEYS), 1)
    row8 = sum((lane8 >= KB * a).astype(jnp.int32) for a in range(1, 5))
    spread = (row8 == lax.broadcasted_iota(jnp.int32, (8, KEYS), 0)).astype(F32)
    for h in range(8):
        mine = metas_ref[zlo * 4 + h // 2, (h % 2) * 8 : (h % 2) * 8 + 8, :]
        vec = lax.dot_general(mine, spread, TN, precision=lax.Precision.HIGHEST, preferred_element_type=F32)
        tile = jnp.full((32, KEYS), NEG, F32)
        for b in range(17):
            tile = jnp.where(delta == b - 8, vec[b : b + 1, :] * LOG2E, tile)
        b_s[h // 2, (h % 2) * 32 : (h % 2) * 32 + 32, :] = tile
    lane128 = lax.broadcasted_iota(jnp.int32, (128, KEYS), 1)
    row128 = sum((lane128 >= KB * a).astype(jnp.int32) for a in range(1, 5))
    pick = (row128 == lax.broadcasted_iota(jnp.int32, (128, KEYS), 0)).astype(F32)
    for z in range(4):
        reach = jnp.dot(metas_ref[z * 4 + ch, 16:24, :], pick, preferred_element_type=F32)
        r_s[z * 8 : z * 8 + 8, :] = reach

    def project(step):
        rows = pl.ds(step * 4, 4)
        parts = []
        for k in range(4):
            p = x_ref[pl.ds(step * 2, 2), k].astype(F32).reshape(2, 14, 2, 8, 128)
            p = jnp.stack([p[r // 2, :, r % 2].reshape(112, 128) for r in range(4)])
            parts.append(p.reshape(448, 128))
        square = jnp.sum(sum(p * p for p in parts), axis=1, keepdims=True)
        scale = lax.rsqrt(square * (1.0 / 512.0) + EPS)
        row = lax.broadcasted_iota(jnp.int32, (448, 1), 0)
        drop = ((step == 0) & (group == 0) & (row < 224)) | ((step == 4) & (group == 15) & (row >= 224))
        normed = jnp.concatenate(
            [
                jnp.where(drop, 0.0, p * scale * metas_ref[zlo * 4 + k, 20:21, :]).astype(BF)
                for k, p in enumerate(parts)
            ],
            axis=1,
        )
        for t, dst, lo, n in ((0, q_s, 8, 96), (1, k_s, 0, 112), (2, v_s, 0, 112)):
            out = jnp.dot(normed, w_s[t], preferred_element_type=F32).reshape(4, 112, 512)[:, lo : lo + n, :]
            if t == 0:
                out = out * (LOG2E / 8.0)
            dst[rows] = out.astype(BF)

    loop(0, 5, project)

    wait_bytes(g_s.at[pl.ds(0, 3)], grsem)
    gained = jnp.concatenate([g_s[k] for k in range(4)], axis=1)
    mixed = jnp.dot(gained, ws_ref[...].astype(BF), preferred_element_type=F32)
    parts = []
    for k in range(3):
        twice = jnp.where((lat + 64 * k) % DEG == 0, 1.0, 2.0).astype(F32)
        parts.append((mixed[k * DEG : k * DEG + DEG] * twice).astype(BF))
    rows_out = lax.dot_general(e_ref[...], jnp.concatenate(parts, axis=0), TN, preferred_element_type=F32)
    send_s[...] = rows_out.astype(BF).reshape(64, 16, 128)
    loop(1, 64, lambda d: remote(send_s.at[(lat + d) % 64], modes_ref.at[lat], assem, arsem, ((lat + d) % 64, ch)))
    acopy = pltpu.make_async_copy(send_s.at[lat], modes_ref.at[lat], lsem.at[0])
    acopy.start()

    left = lax.broadcasted_iota(jnp.int32, (32, 128), 1) < 64
    blocks = [(j, hp) for j in range(3) for hp in range(4)]
    lane1 = row_of[0:1, :]

    def attend_row(i):
        at = group * 16 + i - 2 + lane1
        inside = (at >= 0) & (at < NLAT)
        reach = jnp.where(inside, r_s[pl.ds((i // 4) * 8 + i % 4, 1), :], -1.0)
        allowed = dist <= reach
        for hp in range(4):
            t_s[hp, 0:32, :] = jnp.where(allowed, b_s[hp, 0:32, :], NEG)
            t_s[hp, 32:64, :] = jnp.where(allowed, b_s[hp, 32:64, :], NEG)
        for n, (j, hp) in enumerate(blocks):
            cols = slice(hp * 128, hp * 128 + 128)
            qb = q_s[i + 2, j * 32 : j * 32 + 32, cols]
            zero = jnp.zeros_like(qb)
            qq = jnp.concatenate([jnp.where(left, qb, zero), jnp.where(left, zero, qb)], axis=0)
            kb = k_s[pl.ds(i, 5), j * 32 : j * 32 + KB, cols].reshape(KEYS, 128)
            s_s[n] = lax.dot_general(qq, kb, NT, preferred_element_type=F32) + t_s[hp]
        for n in range(12):
            s = s_s[n]
            p = jnp.exp2(s - jnp.max(s, axis=1, keepdims=True))
            l_s[n] = jnp.broadcast_to(jnp.sum(p, axis=1, keepdims=True), (64, 128))
            p_s[n] = p.astype(BF)
        for n, (j, hp) in enumerate(blocks):
            cols = slice(hp * 128, hp * 128 + 128)
            vb = v_s[pl.ds(i, 5), j * 32 : j * 32 + KB, cols].reshape(KEYS, 128)
            o = jnp.dot(p_s[n], vb, preferred_element_type=F32) / l_s[n]
            a_s[i % 4, j * 32 : j * 32 + 32, cols] = jnp.where(left, o[:32], o[32:]).astype(BF)

    s = win_start(me)
    wide = win_start(me + 1) - s == 12

    def rows_of(step):
        rg = (zlo + step) % 4
        loop(0, 4, lambda r: attend_row(rg * 4 + r))
        out = jnp.dot(a_s[...].reshape(384, 512), w_s[3], preferred_element_type=F32).reshape(2, 2, 12, 8, 512)
        for k in range(4):
            for a in range(2):
                both = jnp.stack([out[a, b, :, :, k * 128 : k * 128 + 128] for b in range(2)], axis=1)
                y_s[rg * 2 + a, k] = both.reshape(12, 16, 128).astype(BF)

        def give(k, n, start):
            start(y_s.at[pl.ds(rg * 2, 2), k, pl.ds(0, n)], out_ref.at[:, pl.ds(s, n)])

        def both(k, start):
            pl.when(wide)(lambda: give(k, 12, start))
            pl.when(jnp.logical_not(wide))(lambda: give(k, 11, start))

        for d in range(1, 4):
            k = (ch + d) % 4
            both(k, lambda a, b, k=k: remote(a, b, ssem, rsem, (group * 4 + rg, k)))
        pl.when(step == 0)(lambda: both(ch, lambda a, b: pltpu.make_async_copy(a, b, lsem.at[1]).start()))
        pl.when(step > 0)(lambda: both(ch, lambda a, b: remote(a, b, ssem, rsem, (group * 4 + rg, ch))))

    loop(0, 4, rows_of)
    acopy.wait()
    wait_bytes(g_s.at[pl.ds(0, 3)], gssem)
    wait_bytes(modes_ref.at[pl.ds(0, 63)], assem)
    wait_bytes(modes_ref.at[pl.ds(0, 63)], arsem)

    def finish(n):
        wait_bytes(out_ref.at[:, pl.ds(0, n)], lsem.at[1])
        wait_bytes(out_ref.at[:, pl.ds(0, 15 * n)], ssem)
        wait_bytes(out_ref.at[:, pl.ds(0, OCT - n)], rsem)

    pl.when(wide)(lambda: finish(12))
    pl.when(jnp.logical_not(wide))(lambda: finish(11))


def attend(*args):
    shape = jax.ShapeDtypeStruct
    return pl.pallas_call(
        attend_kernel,
        out_shape=(shape((2, OCT, 16, 128), BF), shape((64, 16, 128), BF)),
        in_specs=[VMEM] * 7,
        out_specs=[ANY, ANY],
        scratch_shapes=[
            pltpu.VMEM((20, 96, 512), BF),
            pltpu.VMEM((20, 112, 512), BF),
            pltpu.VMEM((20, 112, 512), BF),
            pltpu.VMEM((4, 64, KEYS), F32),
            pltpu.VMEM((4, 64, KEYS), F32),
            pltpu.VMEM((4, 96, 512), BF),
            pltpu.VMEM((12, 64, KEYS), F32),
            pltpu.VMEM((12, 64, KEYS), BF),
            pltpu.VMEM((12, 64, 128), F32),
            pltpu.VMEM((32, KEYS), F32),
            pltpu.VMEM((4, 512, 512), BF),
            pltpu.VMEM((8, 4, 12, 16, 128), BF),
            pltpu.VMEM((4, 3 * DEG, 128), BF),
            pltpu.VMEM((64, 16, 128), BF),
            DMA((2,)), DMA, DMA, DMA, DMA, DMA, DMA,
        ],
        compiler_params=pltpu.CompilerParams(
            collective_id=1, has_side_effects=True, vmem_limit_bytes=48 * 1024 * 1024
        ),
        name="attend",
    )(*args)


def finish_kernel(local_ref, t_ref, got_ref, out_ref):
    modes = lax.dot_general(sort_rows(), got_ref[...].reshape(1024, 128), TN, preferred_element_type=F32).astype(BF)
    for r in range(4):
        wave = lax.dot_general(t_ref[...], modes[r * 192 : r * 192 + 192], TN, preferred_element_type=F32)
        local = local_ref[r // 2].astype(F32).reshape(OCT, 2, 8, 128)[:, r % 2].reshape(NLON, 128)
        out_ref[r] = (wave + local).astype(BF)


def finish(*args):
    return pl.pallas_call(
        finish_kernel,
        out_shape=jax.ShapeDtypeStruct((4, NLON, 128), BF),
        in_specs=[VMEM] * 3,
        out_specs=VMEM,
        compiler_params=pltpu.CompilerParams(vmem_limit_bytes=40 * 1024 * 1024),
        name="finish",
    )(*args)


def small_tables(lat):
    pair = jnp.arange(2 * DEG, dtype=jnp.int32)
    order = (pair % DEG)[:, None]

    def angle(cells):
        return (cells[None, :] * order % NLON).astype(F32) * (2.0 * math.pi / NLON)

    coarse = angle(jnp.arange(128, dtype=jnp.int32) * 128 % NLON)
    fine = angle(jnp.arange(128, dtype=jnp.int32))
    first = (pair < DEG)[:, None]
    cb, sb = jnp.cos(fine), jnp.sin(fine)
    u = jnp.where(first, cb, -sb)
    v = jnp.where(first, -sb, -cb)
    n = jnp.arange(1024, dtype=jnp.int32)
    row = (n // 16) * 4 + n % 4
    theta = (row.astype(F32) + 0.5) * (math.pi / NLAT)
    mine = (lat + 64 * jnp.arange(4, dtype=jnp.int32)) % DEG
    factors = jnp.arange(1, DEG, dtype=F32)
    log_ratio = jnp.log((2.0 * factors - 1.0) / (2.0 * factors))
    log_product = jnp.concatenate([jnp.zeros((1,), F32), jnp.cumsum(log_ratio)])
    orders = jnp.arange(DEG, dtype=F32)
    base = 0.5 * (jnp.log((2.0 * orders + 1.0) / (4.0 * math.pi)) + log_product)
    pick = mine[:, None] == jnp.arange(DEG, dtype=jnp.int32)[None, :]
    start = jnp.sum(jnp.where(pick, base[None, :], 0.0), axis=1)
    kind = (n % 16) // 4
    m = sum(jnp.where(kind == k, mine[k], 0) for k in range(4)).astype(F32)
    begin = sum(jnp.where(kind == k, start[k], 0.0) for k in range(4))
    diagonal = jnp.where(kind < 3, jnp.exp(begin + m * jnp.log(jnp.sin(theta))), 0.0)
    square = lambda a: a.reshape(8, 128)
    return jnp.cos(coarse), jnp.sin(coarse), u, v, square(m), square(diagonal), square(jnp.cos(theta))


def per_device(fields, norm_gain, w_qkv, w_out, rel_bias, stencil_reach, mode_gain, w_spec):
    lat = lax.axis_index("lat")
    weights = jnp.concatenate([jnp.moveaxis(w_qkv, 1, 0), w_out[None]], axis=0)
    weights = lax.all_gather(weights, "ch", axis=0, tiled=False)
    gain = norm_gain.astype(F32)
    bias = jnp.pad(rel_bias, ((0, 0), (0, 3), (0, 111))).reshape(16, 128)
    reach = jnp.pad(stencil_reach.astype(F32), ((0, 0), (0, 123)))
    meta = jnp.concatenate([bias, reach, gain[None], jnp.zeros((3, 128), F32)], axis=0)
    x = fields.astype(F32)
    squares = jnp.sum(x * x, axis=-1)
    colatitude = ((lat * 4 + jnp.arange(4, dtype=jnp.int32)).astype(F32) + 0.5) * (math.pi / NLAT)
    weight = jnp.sin(colatitude) * (math.pi / NLAT * 2.0 * math.pi / NLON)
    gain_weight = weight[:, None] * gain[None, :]
    window, metas, got, legendre, table = gather(fields, squares, meta, gain_weight, *small_tables(lat))
    local, modes = attend(window, metas, weights, got, legendre, mode_gain, w_spec)
    return finish(local, table, modes)


def solution(mesh):
    in_specs = (
        P("lat", None, "ch"),
        P("ch"),
        P(None, None, "ch"),
        P(None, "ch"),
        P("ch", None, None),
        P("lat", None),
        P(None, "ch"),
        P(None, "ch"),
    )
    return jax.shard_map(
        per_device, mesh=mesh, in_specs=in_specs, out_specs=P("lat", None, "ch"), check_vma=False
    )
```

time: 1060 us -> 188 us (0.18)
  waiting for transfers between devices: 559 us -> 0.02 us
  local copies, waits for them, and re-layouts: 185 us -> 5.1 us
  Pallas kernels: 0 us -> 156 us
  matrix products: 123 us -> 0 us
  blocking collectives: 75.2 us -> 0 us
  other arithmetic: 75.7 us -> 12.8 us
  loops' own time: 14.4 us -> 0 us
    reduce_scatter x1 -> x0, waiting for transfers between devices: 257 us -> none  [per_device(): lax.psum_scatter(partial_sums, 'lat', scatter_dimension=0, tiled=True)]
    all_gather x3 -> x1, waiting for transfers between devices: 202 us -> 0.01 us  [per_device(): weights = lax.all_gather(weights, 'ch', axis=0, tiled=False)]
    pallas_call x0 -> x3, Pallas kernels: none -> 156 us  [the longest x1 95.4 us: gather(): pl.pallas_call(gather_kernel, out_shape=(shape((10, 4, 14, 16, 128), BF),...]
    dot_general x25 -> x0, matrix products: 123 us -> none  [the longest x8 50.2 us: attend_row(): jnp.einsum('rbpt,rbtd->bpd', weights, value_win[..., start_ch:stop_ch], p...]
    ppermute x2 -> x0, waiting for transfers between devices: 100 us -> none  [the longest x1 67.5 us: extended_2(): lax.ppermute(head, axis, [((i + 1) % count, i) for i in range(ends)])]
    another operation x79 -> x0, local copies, waits for them, and re-layouts: 79.7 us -> none  [the longest x71 77.6 us: legendre_table(): return jnp.stack(levels, axis=1)]
    all_gather x1 -> x0, blocking collectives: 54.4 us -> none  [per_device(): lax.all_gather(gained.astype(jnp.bfloat16), 'ch', axis=2, tiled=True)]
    reshape x8 -> x1, local copies, waits for them, and re-layouts: 28.1 us -> 0.01 us  [per_device(): bias = jnp.pad(rel_bias, ((0, 0), (0, 3), (0, 111))).reshape(16, 128)]
  transfers between devices with their start and end apart: 6 -> 1, of which waited for: 5 -> 0; matrix products, arithmetic and copies ran while one was open for 35% -> 7% of each run, Pallas kernels for 0% -> 51%
where the time goes in v2:
time: 188 us; the launch traced here: 187 us
  Pallas kernels  156 us (83%)
  between operations  13.5 us (7%)
  other arithmetic  12.8 us (7%)
  local copies, waits for them, and re-layouts  5.1 us (3%)
    pallas_call x1, Pallas kernels, gather(): pl.pallas_call(gather_kernel, out_shape=(shape((10, 4, 14, 16, 128), BF),...  95.4 us
    pallas_call x1, Pallas kernels, attend(): pl.pallas_call(attend_kernel, out_shape=(shape((2, OCT, 16, 128), BF), sh...  57.3 us
    select_n x1, other arithmetic, small_tables(): jnp.where(kind < 3, jnp.exp(begin + m * jnp.log(jnp.sin(theta))), 0.0)  5.04 us
  transfers between devices with their start and end apart: 1, of which 0 were waited for; matrix products, arithmetic and copies ran while one was open for 7% of the time, Pallas kernels for 51%

profile of v2, /device:TPU:1, one launch (start us, length us, event | category | flops | bytes accessed | tf_op | source)
XLA Modules:
  0.0 187.5 jit_solution(9254745103135669357)
XLA Ops:
  6.5 0.0 copy-start
  6.5 0.0 copy-start.5
  6.5 0.0 all-gather.3.cloned.1.call-start
  6.5 2.0 %pad_maximum_fusion = bf16[4,512,128]{2,1,0:T(8,128)(2,1)} fusion(bf16[1,512,128]{2,1,0:T(8,128)(2,1)} %bitcast.17, bf16[3,512,128]{2,1,0:T(8,128)(2,1)} %bitcast.16), kind=kLoop, calls=%fused_computation.1 | loop fusion | flops 262144 | bytes 1048576 | tf_op jit(solution)/shard_map/concatenate | solution.py:484
  8.6 0.0 all-gather.3.cloned.1.call-update
  8.6 0.0 copy-start.3
  8.6 0.0 copy-start.4
  8.6 0.7 convert_element_type.43
  9.3 0.7 copy.13
  10.1 0.1 reduce-window.8
  10.2 0.1 pad.17.clone
  10.3 0.1 reduce
  10.5 0.1 fusion.32
  10.6 0.7 fusion.34
  11.2 2.4 %add_convert_fusion.m_ref = f32[8,128]{1,0:T(8,128)S(1)} fusion(s32[]{:T(128)} %bitcast.5, s32[]{:T(128)} %bitcast.4, s32[]{:T(128)} %bitcast.3, s32[]{:T(128)} %bitcast.2), kind=kLoop, calls=%fused_computation.50 | loop fusion | flops 40960 | bytes 4112 | tf_op jit(solution)/shard_map/convert_element_type | solution.py:475
  13.7 0.2 select_reduce_fusion
  13.9 0.7 fusion.33
  14.5 5.0 %exponential_select_fusion = (f32[8,128]{1,0:T(8,128)S(1)}, f32[8,128]{1,0:T(8,128)S(1)}) fusion(f32[]{:T(128)} %bitcast.9, f32[]{:T(128)} %bitcast.8, f32[]{:T(128)} %bitcast.7, f32[]{:T(128)} %bitcast.6, s32[]{:T(128)} %bitcast.5, s32[]{:T(128)} %bitcast.4, s32[]{:T(128)} %bitcast.3, s32[]{:T(128)} %bitcast.2), kind=kLoop, calls=%fused_computation.48 | loop fusion | flops 73728 | bytes 8224 | tf_op jit(solution)/shard_map/jit(_where)/select_n | solution.py:477
  19.6 0.0 copy-done
  19.6 0.9 multiply_reduce_fusion.sq_ref
  20.5 0.0 copy-done.5
  20.5 0.1 broadcast_multiply_fusion.gw_ref
  20.6 0.1 fusion.16.meta_ref
  20.7 0.9 negate_select_fusion
  21.6 95.4 %gather.1 = (bf16[10,4,14,16,128]{4,3,2,1,0:T(8,128)(2,1)S(1)}, f32[16,24,128]{2,1,0:T(8,128)S(1)}, bf16[64,16,128]{2,1,0:T(8,128)(2,1)S(1)}, bf16[288,1024]{1,0:T(8,128)(2,1)S(1)}, bf16[192,1440]{1,0:T(8,128)(2,1)S(1)}) custom-call(bf16[4,1440,128]{2,1,0:T(8,128)(2,1)S(1)} %copy-done, f32[4,1440]{1,0:T(4,128)S(1)} %multiply_reduce_fusion.sq_ref, ...), custom_call_target="tpu_custom_call" | custom-call | tf_op jit(solution)/shard_map/gather/pallas_call | solution.py:221
  117.0 0.0 copy-start.1
  117.0 1.4 copy-done.1
  118.4 0.0 copy-done.3
  118.4 0.0 copy-done.4
  118.4 1.6 copy-done.2
  120.0 57.3 %attend.1 = (bf16[2,180,16,128]{3,2,1,0:T(8,128)(2,1)S(1)}, bf16[64,16,128]{2,1,0:T(8,128)(2,1)S(1)}) custom-call(bf16[10,4,14,16,128]{4,3,2,1,0:T(8,128)(2,1)} %copy-done.1, f32[16,24,128]{2,1,0:T(8,128)S(1)} %get-tuple-element.13.metas_ref, bf16[4,4,512,128]{3,2,1,0:T(8,128)(2,1)S(1)} %bitcast.15, bf16[64,16,128]{2,1,0:T(8,128)(2,1)S(1)} %get-tuple-element.14.got_ref, ...), custom_call_target="tpu_custom_call" | custom-call | tf_op jit(solution)/shard_map/attend/pallas_call | solution.py:402
  177.2 3.4 %finish.1 = bf16[4,1440,128]{2,1,0:T(8,128)(2,1)} custom-call(bf16[2,180,16,128]{3,2,1,0:T(8,128)(2,1)S(1)} %get-tuple-element.16.local_ref, bf16[192,1440]{1,0:T(8,128)(2,1)S(1)} %get-tuple-element.17.t_ref, bf16[64,16,128]{2,1,0:T(8,128)(2,1)S(1)} %get-tuple-element.18.got_ref), custom_call_target="tpu_custom_call" | custom-call | tf_op jit(solution)/shard_map/finish/pallas_call | solution.py:440
  (11 shorter events, 0.1 us)
Async XLA Ops:
  6.5 13.1 %copy-start = (bf16[4,1440,128]{2,1,0:T(8,128)(2,1)S(1)}, bf16[4,1440,128]{2,1,0:T(8,128)(2,1)}, u32[]{:S(2)}) copy-start(bf16[4,1440,128]{2,1,0:T(8,128)(2,1)} %f_ref.1) | copy-start | bytes 4423684
  6.5 14.0 %copy-start.5 = (bf16[128]{0:T(256)(128)(2,1)S(1)}, bf16[128]{0:T(256)(128)(2,1)}, u32[]{:S(2)}) copy-start(bf16[128]{0:T(256)(128)(2,1)} %param.9) | copy-start | bytes 772
  6.5 111.8 %all-gather.3.cloned.1.call-start = ((), (), s32[]{:S(2)}) async-start(), calls=%async_computation | async-start | bytes 2621440 | tf_op jit(solution)/shard_map/all_gather | solution.py:485
  8.6 109.8 %copy-start.3 = (f32[512,128]{1,0:T(8,128)S(1)}, f32[512,128]{1,0:T(8,128)}, u32[]{:S(2)}) copy-start(f32[512,128]{1,0:T(8,128)} %ws_ref.1) | copy-start | bytes 786436
  8.6 109.8 %copy-start.4 = (f32[96,128]{1,0:T(8,128)S(1)}, f32[96,128]{1,0:T(8,128)}, u32[]{:S(2)}) copy-start(f32[96,128]{1,0:T(8,128)} %mg_ref.1) | copy-start | bytes 147460
  117.0 1.4 copy-start.1
  118.4 1.6 copy-start.2
Sparse Core Ops, SparseCore 0:
  9.2 59.3 all-gather.2

commit v3 on v2

v3 whole, which is shorter than its diff:
```python
import math

import jax
import jax.numpy as jnp
from jax import lax
from jax.experimental import pallas as pl
from jax.experimental.pallas import tpu as pltpu
from jax.sharding import PartitionSpec as P

MESH = pl.DeviceIdType.MESH
NLON = 1440
NLAT = 256
DEG = 96
OCT = 180
LOG2E = 1.4426950408889634
NEG = -1e30
EPS = 1e-05
KB = 48
KEYS = 5 * KB
F32 = jnp.float32
BF = jnp.bfloat16
DMA = pltpu.SemaphoreType.DMA
VMEM = pl.BlockSpec(memory_space=pltpu.VMEM)
ANY = pl.BlockSpec(memory_space=pl.ANY)
TN = (((0,), (0,)), ((), ()))
NT = (((1,), (1,)), ((), ()))


def win_start(w):
    return 45 * w // 4


def ring_dev(w, group):
    return (group * 4 + w // 4, w % 4)


def place():
    lat = lax.axis_index("lat")
    ch = lax.axis_index("ch")
    return lat, ch, lat // 4, lat % 4


def signal(device):
    pl.semaphore_signal(pltpu.get_barrier_semaphore(), inc=1, device_id=device, device_id_type=MESH)


def remote(src, dst, ss, rs, device):
    pltpu.make_async_remote_copy(
        src_ref=src, dst_ref=dst, send_sem=ss, recv_sem=rs, device_id=device, device_id_type=MESH
    ).start()


def wait_bytes(ref, sem):
    pltpu.make_async_copy(ref, ref, sem).wait()


def loop(lo, hi, body):
    def step(i, c):
        body(i)
        return c

    lax.fori_loop(lo, hi, step, 0)


def sort_rows():
    n = lax.broadcasted_iota(jnp.int32, (1024, 1), 0)
    slot = n % 16
    source = jnp.where(slot < 12, (slot % 4) * 192 + (slot // 4) * 64 + n // 16, -1)
    return (lax.broadcasted_iota(jnp.int32, (1024, 768), 1) == source).astype(F32).astype(BF)


def tables(tab_s, t_ref):
    row = lax.broadcasted_iota(jnp.int32, (2 * DEG, 128), 0)
    lane = lax.broadcasted_iota(jnp.int32, (2 * DEG, 128), 1).astype(F32)
    first = row < DEG
    order = jnp.where(first, row, row - DEG).astype(F32)

    def angle(cells):
        turns = cells * order
        turns = turns - NLON * jnp.floor((turns + 0.5) * (1.0 / NLON))
        return turns * (2.0 * math.pi / NLON)

    coarse, fine = angle(jnp.where(lane < 12, lane * 128.0, 0.0)), angle(lane)
    ca, sa, cb, sb = jnp.cos(coarse), jnp.sin(coarse), jnp.cos(fine), jnp.sin(fine)
    u = jnp.where(first, cb, -sb)
    v = jnp.where(first, -sb, -cb)
    for a in range(12):
        n = min(128, NLON - a * 128)
        tab = ca[:, a : a + 1] * u + sa[:, a : a + 1] * v
        tab_s[:, a * 128 : a * 128 + n] = tab[:, :n]
        t_ref[:, a * 128 : a * 128 + n] = tab[:, :n].astype(BF)


def legendre(lat, leg_s, e_s):
    lane = lax.broadcasted_iota(jnp.int32, (8, 128), 1)
    n = lax.broadcasted_iota(jnp.int32, (8, 128), 0) * 128 + lane
    kind = (n % 16) // 4
    row = (n // 16) * 4 + n % 4
    theta = (row.astype(F32) + 0.5) * (math.pi / NLAT)
    factor = lax.broadcasted_iota(jnp.int32, (1, 128), 1)
    number = jnp.maximum(factor, 1).astype(F32)
    log_ratio = jnp.log((2.0 * number - 1.0) / (2.0 * number))
    m = jnp.zeros((8, 128), F32)
    begin = jnp.zeros((8, 128), F32)
    for k in range(3):
        order = (lat + 64 * k) % DEG
        total = jnp.sum(jnp.where((factor >= 1) & (factor <= order), log_ratio, 0.0), axis=1, keepdims=True)
        m = jnp.where(kind == k, order.astype(F32), m)
        begin = jnp.where(kind == k, total, begin)
    begin = 0.5 * (begin + jnp.log((2.0 * m + 1.0) / (4.0 * math.pi)))
    diagonal = jnp.where(kind < 3, jnp.exp(begin + m * jnp.log(jnp.sin(theta))), 0.0)
    cosine = jnp.cos(theta)

    def degree(l, carry):
        previous, earlier = carry
        deg = l.astype(F32)
        less = deg - 1.0
        upper = jnp.sqrt(jnp.maximum(4.0 * deg * deg - 1.0, 0.0) / jnp.maximum(deg * deg - m * m, 1.0))
        lower = jnp.sqrt(jnp.maximum(less * less - m * m, 0.0) / jnp.maximum(4.0 * less * less - 1.0, 1.0))
        value = upper * (cosine * previous - lower * earlier)
        current = jnp.where(m == deg, diagonal, jnp.where(m < deg, value, 0.0))
        leg_s[l] = current
        return current, previous

    zero = diagonal * 0.0
    lax.fori_loop(0, DEG, degree, (zero, zero))
    kind = (lax.broadcasted_iota(jnp.int32, (DEG, 128), 1) % 16) // 4
    for c in range(8):
        part = leg_s[:, c, :]
        for k in range(3):
            e_s[k * DEG : k * DEG + DEG, c * 128 : c * 128 + 128] = jnp.where(kind == k, part, 0.0).astype(BF)


def layer_kernel(
    f_ref, sq_ref, gain_ref, wq_ref, wo_ref, bias_ref, reach_ref, mg_ref, ws_ref,
    out_ref, modes_ref, t_ref,
    x_s, win_s, w_s, meta_s, metas_s, stat_s, tab_s, leg_s, e_s, send1_s, got_s, g_s, send2_s,
    q_s, k_s, v_s, b_s, t_s, a_s, s_s, p_s, l_s, r_s, y_s,
    lsem, statsem, metasem, w1sem, wbsem, w2sem, ssem, usem, nsem, hsem, a1sem, a2sem, gsem, bsem,
):
    lat, ch, group, zlo = place()
    me = zlo * 4 + ch
    has_next = group < 15
    has_prev = group > 0
    quarter = pl.ds(pl.multiple_of((group // 4) * 128, 128), 128)
    sib = ch + 1 - 2 * (ch % 2)
    across = (ch + 2) % 4
    loop(1, 64, lambda d: signal(((lat + d) % 64, ch)))
    for z in range(4):
        for d in range(1, 4):
            signal((group * 4 + z, (ch + d) % 4))
    for d in range(1, 4):
        signal(((lat + 16 * d) % 64, sib))

    stat_s[ch] = sq_ref[...]
    gain = gain_ref[...].astype(F32)
    meta_s[...] = jnp.zeros_like(meta_s)
    for a in range(5):
        for h in range(2):
            meta_s[h * 8 + a : h * 8 + a + 1, 0:17] = bias_ref[a, h : h + 1, :]
    meta_s[16:20, 0:5] = reach_ref[...].astype(F32)
    meta_s[20:21, :] = gain

    def interleave(c):
        lon = pl.ds(pl.multiple_of(c * 144, 16), 144)
        for a in range(2):
            two = [f_ref[2 * a + b, lon, :].astype(F32).reshape(18, 8, 128) for b in range(2)]
            x_s[a, pl.ds(c * 18, 18)] = jnp.stack(two, axis=1).reshape(18, 16, 128).astype(BF)

    loop(0, 10, interleave)

    @pl.when(jnp.logical_not(has_prev))
    def _():
        win_s[0] = jnp.zeros_like(win_s[0])

    @pl.when(jnp.logical_not(has_next))
    def _():
        win_s[9] = jnp.zeros_like(win_s[9])

    pl.semaphore_wait(pltpu.get_barrier_semaphore(), 78)

    for d in range(1, 4):
        remote(sq_ref, stat_s.at[ch], statsem.at[0], statsem.at[1], (lat, (ch + d) % 4))
    for d in range(1, 4):
        remote(meta_s, metas_s.at[me], metasem.at[0], metasem.at[1], (lat, (ch + d) % 4))
        remote(meta_s, metas_s.at[me], metasem.at[0], metasem.at[1], (group * 4 + (zlo + d) % 4, ch))
    remote(wq_ref.at[:, quarter], w_s.at[pl.ds(ch * 4, 3), quarter], w1sem.at[0], w1sem.at[1], (lat, across))
    remote(wo_ref.at[quarter], w_s.at[ch * 4 + 3, quarter], w1sem.at[0], w1sem.at[1], (lat, across))
    remote(wq_ref, w_s.at[pl.ds(ch * 4, 3)], wbsem.at[0], wbsem.at[1], (lat, sib))
    remote(wo_ref, w_s.at[ch * 4 + 3], wbsem.at[0], wbsem.at[1], (lat, sib))
    own = [
        pltpu.make_async_copy(meta_s, metas_s.at[me], lsem.at[2]),
        pltpu.make_async_copy(wq_ref, w_s.at[pl.ds(ch * 4, 3)], lsem.at[3]),
        pltpu.make_async_copy(wo_ref, w_s.at[ch * 4 + 3], lsem.at[4]),
    ]
    for copy in own:
        copy.start()

    def move(w, src_pair, pairs, dst_pair, start):
        s = win_start(w)
        src, dst = pl.ds(src_pair, pairs), pl.ds(dst_pair, pairs)
        edge = (w == 0) | (w == 15)

        @pl.when(edge)
        def _():
            a_src = jnp.where(w == 0, 0, s - 1)
            a_dst = jnp.where(w == 0, 1, 0)
            b_src = jnp.where(w == 0, OCT - 1, 0)
            b_dst = jnp.where(w == 0, 0, 13)
            start(x_s.at[src, pl.ds(a_src, 13)], win_s.at[dst, ch, pl.ds(a_dst, 13)], 0)
            start(x_s.at[src, pl.ds(b_src, 1)], win_s.at[dst, ch, pl.ds(b_dst, 1)], 1)

        @pl.when(jnp.logical_not(edge))
        def _():
            start(x_s.at[src, pl.ds(s - 1, 14)], win_s.at[dst, ch], 0)

    def spread(pair, ss, rs):
        def one(d):
            w = (me + d) % 16
            move(w, pair, 1, 1 + 2 * zlo + pair, lambda a, b, n: remote(a, b, ss, rs, ring_dev(w, group)))

        loop(1, 16, one)

    move(me, 0, 2, 1 + 2 * zlo, lambda a, b, n: pltpu.make_async_copy(a, b, lsem.at[n]).start())
    urgent = jnp.where(zlo == 3, 1, 0)
    spread(urgent, ssem.at[0], usem.at[jnp.where(zlo == 0, 1, jnp.where(zlo == 3, 2, 0))])

    tables(tab_s, t_ref)
    wait_bytes(stat_s.at[pl.ds(0, 3)], statsem.at[1])
    scale = lax.rsqrt((stat_s[0] + stat_s[1] + stat_s[2] + stat_s[3]) * (1.0 / 512.0) + EPS)
    theta = ((lat * 4 + lax.broadcasted_iota(jnp.int32, (4, 128), 0)).astype(F32) + 0.5) * (math.pi / NLAT)
    weight = jnp.sin(theta) * (math.pi / NLAT * 2.0 * math.pi / NLON) * gain
    freq = []
    for r in range(4):
        lhs = (tab_s[...] * scale[r : r + 1, :]).astype(BF)
        out = jnp.dot(lhs, f_ref[r], preferred_element_type=F32)
        freq.append((out * weight[r : r + 1, :]).astype(BF))
    out = jnp.dot(sort_rows(), jnp.concatenate(freq, axis=0), preferred_element_type=F32)
    send1_s[...] = out.astype(BF).reshape(64, 16, 128)
    loop(1, 64, lambda d: remote(send1_s.at[(lat + d) % 64], got_s.at[lat], a1sem.at[0], a1sem.at[1], ((lat + d) % 64, ch)))
    got_s[lat] = send1_s[lat]

    spread(1 - urgent, ssem.at[1], nsem)

    part = w_s.at[pl.ds(across * 4, 4), quarter]
    wait_bytes(part, w1sem.at[1])
    remote(part, part, w2sem.at[0], w2sem.at[1], (lat, sib))
    for d in range(1, 4):
        remote(part, part, w2sem.at[0], w2sem.at[1], ((lat + 16 * d) % 64, ch))
        remote(part, part, w2sem.at[0], w2sem.at[1], ((lat + 16 * d) % 64, sib))

    legendre(lat, leg_s, e_s)

    for copy in own:
        copy.wait()
    wait_bytes(metas_s.at[pl.ds(0, 6)], metasem.at[1])
    lane = lax.broadcasted_iota(jnp.int32, (32, KEYS), 1)
    query = lax.broadcasted_iota(jnp.int32, (32, KEYS), 0)
    row_of = sum((lane >= KB * a).astype(jnp.int32) for a in range(1, 5))
    delta = lane - KB * row_of - query - 8
    dist = jnp.abs(delta).astype(F32)
    lane8 = lax.broadcasted_iota(jnp.int32, (8, KEYS), 1)
    row8 = sum((lane8 >= KB * a).astype(jnp.int32) for a in range(1, 5))
    onto = (row8 == lax.broadcasted_iota(jnp.int32, (8, KEYS), 0)).astype(F32)
    for h in range(8):
        mine = metas_s[zlo * 4 + h // 2, (h % 2) * 8 : (h % 2) * 8 + 8, :]
        vec = lax.dot_general(mine, onto, TN, precision=lax.Precision.HIGHEST, preferred_element_type=F32)
        tile = jnp.full((32, KEYS), NEG, F32)
        for b in range(17):
            tile = jnp.where(delta == b - 8, vec[b : b + 1, :] * LOG2E, tile)
        b_s[h // 2, (h % 2) * 32 : (h % 2) * 32 + 32, :] = tile
    lane128 = lax.broadcasted_iota(jnp.int32, (128, KEYS), 1)
    row128 = sum((lane128 >= KB * a).astype(jnp.int32) for a in range(1, 5))
    pick = (row128 == lax.broadcasted_iota(jnp.int32, (128, KEYS), 0)).astype(F32)
    for z in range(4):
        r_s[z * 8 : z * 8 + 8, :] = jnp.dot(metas_s[z * 4 + ch, 16:24, :], pick, preferred_element_type=F32)

    @pl.when((me == 0) | (me == 15))
    def _():
        wait_bytes(win_s.at[pl.ds(0, 2), 0, pl.ds(0, 13)], lsem.at[0])
        wait_bytes(win_s.at[pl.ds(0, 2), 0, pl.ds(0, 1)], lsem.at[1])

    @pl.when((me != 0) & (me != 15))
    def _():
        wait_bytes(win_s.at[pl.ds(0, 2), 0], lsem.at[0])

    def arrived(own_here, full, sem):
        pl.when(own_here)(lambda: wait_bytes(win_s.at[pl.ds(0, full - 1), 0], sem))
        pl.when(jnp.logical_not(own_here))(lambda: wait_bytes(win_s.at[pl.ds(0, full), 0], sem))

    arrived(zlo == 0, 4, usem.at[1])
    arrived(zlo == 3, 4, usem.at[2])
    pl.when(has_next)(lambda: remote(win_s.at[8], win_s.at[0], hsem.at[0], hsem.at[1], ((lat + 4) % 64, ch)))
    pl.when(has_prev)(lambda: remote(win_s.at[1], win_s.at[9], hsem.at[2], hsem.at[3], ((lat + 60) % 64, ch)))

    wait_bytes(got_s.at[pl.ds(0, 63)], a1sem.at[1])
    coef = jnp.dot(e_s[...], got_s[...].reshape(1024, 128), preferred_element_type=F32)
    coef = coef.reshape(3, DEG, 128) * mg_ref[...][None]
    g_s[ch] = coef.reshape(3 * DEG, 128).astype(BF)
    for d in range(1, 4):
        remote(g_s.at[ch], g_s.at[ch], gsem.at[0], gsem.at[1], (lat, (ch + d) % 4))

    def weights(t):
        return jnp.concatenate([w_s[k * 4 + t] for k in range(4)], axis=1)

    def project(pair, inner):
        parts = []
        for k in range(4):
            p = win_s[pair, k].astype(F32).reshape(14, 2, 8, 128)
            parts.append(jnp.concatenate([p[:, r].reshape(112, 128) for r in range(2)], axis=0))
        square = jnp.sum(sum(p * p for p in parts), axis=1, keepdims=True)
        scale = lax.rsqrt(square * (1.0 / 512.0) + EPS)
        normed = jnp.concatenate(
            [(p * scale * metas_s[zlo * 4 + k, 20:21, :]).astype(BF) for k, p in enumerate(parts)], axis=1
        )
        rows = pl.ds(pair * 2, 2)
        for t, dst, lo, n in ((0, q_s, 8, 96), (1, k_s, 0, 112), (2, v_s, 0, 112)):
            if t == 0 and not inner:
                continue
            out = jnp.dot(normed, weights(t), preferred_element_type=F32).reshape(2, 112, 512)[:, lo : lo + n, :]
            if t == 0:
                out = out * (LOG2E / 8.0)
            dst[rows] = out.astype(BF)

    wait_bytes(w_s.at[pl.ds(0, 4)], wbsem.at[1])
    wait_bytes(w_s.at[pl.ds(0, 7)], w2sem.at[1])
    arrived((zlo == 1) | (zlo == 2), 8, usem.at[0])
    loop(0, 4, lambda i: project(1 + 2 * i + i // 3, True))

    wait_bytes(g_s.at[pl.ds(0, 3)], gsem.at[1])
    gained = jnp.concatenate([g_s[k] for k in range(4)], axis=1)
    mixed = jnp.dot(gained, ws_ref[...].astype(BF), preferred_element_type=F32)
    parts = []
    for k in range(3):
        twice = jnp.where((lat + 64 * k) % DEG == 0, 1.0, 2.0).astype(F32)
        parts.append((mixed[k * DEG : k * DEG + DEG] * twice).astype(BF))
    rows_out = lax.dot_general(e_s[...], jnp.concatenate(parts, axis=0), TN, preferred_element_type=F32)
    send2_s[...] = rows_out.astype(BF).reshape(64, 16, 128)
    loop(1, 64, lambda d: remote(send2_s.at[(lat + d) % 64], modes_ref.at[lat], a2sem.at[0], a2sem.at[1], ((lat + d) % 64, ch)))
    acopy = pltpu.make_async_copy(send2_s.at[lat], modes_ref.at[lat], lsem.at[5])
    acopy.start()

    wait_bytes(win_s.at[pl.ds(0, 5), pl.ds(0, 3)], nsem)
    loop(0, 4, lambda i: project(2 + 2 * i - i // 3, True))
    pl.when(has_prev)(lambda: wait_bytes(win_s.at[0], hsem.at[1]))
    project(0, False)
    pl.when(has_next)(lambda: wait_bytes(win_s.at[0], hsem.at[3]))
    project(9, False)

    left = lax.broadcasted_iota(jnp.int32, (32, 128), 1) < 64
    blocks = [(j, hp) for j in range(3) for hp in range(4)]
    lane1 = row_of[0:1, :]

    def attend_row(i):
        at = group * 16 + i - 2 + lane1
        inside = (at >= 0) & (at < NLAT)
        reach = jnp.where(inside, r_s[pl.ds((i // 4) * 8 + i % 4, 1), :], -1.0)
        allowed = dist <= reach
        for hp in range(4):
            t_s[hp, 0:32, :] = jnp.where(allowed, b_s[hp, 0:32, :], NEG)
            t_s[hp, 32:64, :] = jnp.where(allowed, b_s[hp, 32:64, :], NEG)
        for n, (j, hp) in enumerate(blocks):
            cols = slice(hp * 128, hp * 128 + 128)
            qb = q_s[i + 2, j * 32 : j * 32 + 32, cols]
            zero = jnp.zeros_like(qb)
            qq = jnp.concatenate([jnp.where(left, qb, zero), jnp.where(left, zero, qb)], axis=0)
            kb = k_s[pl.ds(i, 5), j * 32 : j * 32 + KB, cols].reshape(KEYS, 128)
            s_s[n] = lax.dot_general(qq, kb, NT, preferred_element_type=F32) + t_s[hp]
        for n in range(12):
            s = s_s[n]
            p = jnp.exp2(s - jnp.max(s, axis=1, keepdims=True))
            l_s[n] = jnp.broadcast_to(jnp.sum(p, axis=1, keepdims=True), (64, 128))
            p_s[n] = p.astype(BF)
        for n, (j, hp) in enumerate(blocks):
            cols = slice(hp * 128, hp * 128 + 128)
            vb = v_s[pl.ds(i, 5), j * 32 : j * 32 + KB, cols].reshape(KEYS, 128)
            o = jnp.dot(p_s[n], vb, preferred_element_type=F32) / l_s[n]
            a_s[i % 4, j * 32 : j * 32 + 32, cols] = jnp.where(left, o[:32], o[32:]).astype(BF)

    s = win_start(me)
    wide = win_start(me + 1) - s == 12

    def rows_of(step):
        rg = (zlo + step) % 4
        loop(0, 4, lambda r: attend_row(rg * 4 + r))
        out = jnp.dot(a_s[...].reshape(384, 512), weights(3), preferred_element_type=F32).reshape(2, 2, 12, 8, 512)
        for k in range(4):
            for a in range(2):
                both = jnp.stack([out[a, b, :, :, k * 128 : k * 128 + 128] for b in range(2)], axis=1)
                y_s[rg * 2 + a, k] = both.reshape(12, 16, 128).astype(BF)

        def give(k, n, start):
            start(y_s.at[pl.ds(rg * 2, 2), k, pl.ds(0, n)], out_ref.at[:, pl.ds(s, n)])

        def both(k, start):
            pl.when(wide)(lambda: give(k, 12, start))
            pl.when(jnp.logical_not(wide))(lambda: give(k, 11, start))

        for d in range(1, 4):
            k = (ch + d) % 4
            both(k, lambda a, b, k=k: remote(a, b, bsem.at[0], bsem.at[1], (group * 4 + rg, k)))
        pl.when(step == 0)(lambda: both(ch, lambda a, b: pltpu.make_async_copy(a, b, lsem.at[6]).start()))
        pl.when(step > 0)(
            lambda: both(ch, lambda a, b: remote(a, b, bsem.at[0], bsem.at[1], (group * 4 + rg, ch)))
        )

    loop(0, 4, rows_of)

    wait_bytes(stat_s.at[pl.ds(0, 3)], statsem.at[0])
    wait_bytes(metas_s.at[pl.ds(0, 6)], metasem.at[0])
    wait_bytes(part, w1sem.at[0])
    wait_bytes(w_s.at[pl.ds(0, 4)], wbsem.at[0])
    wait_bytes(w_s.at[pl.ds(0, 7)], w2sem.at[0])
    wait_bytes(win_s.at[pl.ds(0, 5), pl.ds(0, 3)], ssem.at[0])
    wait_bytes(win_s.at[pl.ds(0, 5), pl.ds(0, 3)], ssem.at[1])
    pl.when(has_next)(lambda: wait_bytes(win_s.at[0], hsem.at[0]))
    pl.when(has_prev)(lambda: wait_bytes(win_s.at[0], hsem.at[2]))
    wait_bytes(got_s.at[pl.ds(0, 63)], a1sem.at[0])
    wait_bytes(g_s.at[pl.ds(0, 3)], gsem.at[0])
    acopy.wait()
    wait_bytes(modes_ref.at[pl.ds(0, 63)], a2sem.at[0])
    wait_bytes(modes_ref.at[pl.ds(0, 63)], a2sem.at[1])

    def last(n):
        wait_bytes(out_ref.at[:, pl.ds(0, n)], lsem.at[6])
        wait_bytes(out_ref.at[:, pl.ds(0, 15 * n)], bsem.at[0])
        wait_bytes(out_ref.at[:, pl.ds(0, OCT - n)], bsem.at[1])

    pl.when(wide)(lambda: last(12))
    pl.when(jnp.logical_not(wide))(lambda: last(11))


def layer(*args):
    shape = jax.ShapeDtypeStruct
    vm = pltpu.VMEM
    return pl.pallas_call(
        layer_kernel,
        out_shape=(shape((2, OCT, 16, 128), BF), shape((64, 16, 128), BF), shape((2 * DEG, NLON), BF)),
        in_specs=[VMEM] * 9,
        out_specs=[ANY, ANY, VMEM],
        scratch_shapes=[
            vm((2, OCT, 16, 128), BF),
            vm((10, 4, 14, 16, 128), BF),
            vm((16, 512, 128), BF),
            vm((24, 128), F32),
            vm((16, 24, 128), F32),
            vm((4, 4, NLON), F32),
            vm((2 * DEG, NLON), F32),
            vm((DEG, 8, 128), F32),
            vm((3 * DEG, 1024), BF),
            vm((64, 16, 128), BF),
            vm((64, 16, 128), BF),
            vm((4, 3 * DEG, 128), BF),
            vm((64, 16, 128), BF),
            vm((20, 96, 512), BF),
            vm((20, 112, 512), BF),
            vm((20, 112, 512), BF),
            vm((4, 64, KEYS), F32),
            vm((4, 64, KEYS), F32),
            vm((4, 96, 512), BF),
            vm((12, 64, KEYS), F32),
            vm((12, 64, KEYS), BF),
            vm((12, 64, 128), F32),
            vm((32, KEYS), F32),
            vm((8, 4, 12, 16, 128), BF),
            DMA((7,)), DMA((2,)), DMA((2,)), DMA((2,)), DMA((2,)), DMA((2,)), DMA((2,)), DMA((3,)), DMA,
            DMA((4,)), DMA((2,)), DMA((2,)), DMA((2,)), DMA((2,)),
        ],
        compiler_params=pltpu.CompilerParams(
            collective_id=0, has_side_effects=True, vmem_limit_bytes=56 * 1024 * 1024
        ),
        name="layer",
    )(*args)


def finish_kernel(local_ref, t_ref, got_ref, out_ref):
    modes = lax.dot_general(sort_rows(), got_ref[...].reshape(1024, 128), TN, preferred_element_type=F32).astype(BF)
    for r in range(4):
        wave = lax.dot_general(t_ref[...], modes[r * 192 : r * 192 + 192], TN, preferred_element_type=F32)
        local = local_ref[r // 2].astype(F32).reshape(OCT, 2, 8, 128)[:, r % 2].reshape(NLON, 128)
        out_ref[r] = (wave + local).astype(BF)


def finish(*args):
    return pl.pallas_call(
        finish_kernel,
        out_shape=jax.ShapeDtypeStruct((4, NLON, 128), BF),
        in_specs=[VMEM] * 3,
        out_specs=VMEM,
        compiler_params=pltpu.CompilerParams(vmem_limit_bytes=40 * 1024 * 1024),
        name="finish",
    )(*args)


def per_device(fields, norm_gain, w_qkv, w_out, rel_bias, stencil_reach, mode_gain, w_spec):
    x = fields.astype(F32)
    squares = jnp.sum(x * x, axis=-1)
    local, modes, table = layer(
        fields,
        squares,
        norm_gain.reshape(1, 128),
        jnp.transpose(w_qkv, (1, 0, 2)),
        w_out,
        jnp.transpose(rel_bias, (1, 0, 2)),
        stencil_reach,
        mode_gain,
        w_spec,
    )
    return finish(local, table, modes)


def solution(mesh):
    in_specs = (
        P("lat", None, "ch"),
        P("ch"),
        P(None, None, "ch"),
        P(None, "ch"),
        P("ch", None, None),
        P("lat", None),
        P(None, "ch"),
        P(None, "ch"),
    )
    return jax.shard_map(
        per_device, mesh=mesh, in_specs=in_specs, out_specs=P("lat", None, "ch"), check_vma=False
    )
```

time: 188 us -> 127 us (0.68)
  Pallas kernels: 156 us -> 119 us
  between operations: 13.5 us -> 0.02 us
  other arithmetic: 12.8 us -> 2.88 us
    pallas_call x2 -> x1, Pallas kernels: 153 us -> 115 us  [layer(): pl.pallas_call(layer_kernel, out_shape=(shape((2, OCT, 16, 128), BF), sha...]
    select_n x5 -> x0, other arithmetic: 5.98 us -> none  [the longest x1 5.04 us: small_tables(): jnp.where(kind < 3, jnp.exp(begin + m * jnp.log(jnp.sin(theta))), 0.0)]
    convert_element_type x3 -> x0, other arithmetic: 3.17 us -> none  [the longest x1 2.44 us: small_tables(): m = sum((jnp.where(kind == k, mine[k], 0) for k in range(4))).astype(F32)]
    concatenate x2 -> x0, other arithmetic: 2.08 us -> none  [the longest x1 2.01 us: per_device(): weights = jnp.concatenate([jnp.moveaxis(w_qkv, 1, 0), w_out[None]], axis=0)]
    reduce_sum x1, other arithmetic: 0.91 us -> 2.88 us  [per_device(): squares = jnp.sum(x * x, axis=-1)]
  transfers between devices with their start and end apart: 1 -> 0, of which waited for: 0 -> 0; matrix products, arithmetic and copies ran while one was open for 7% -> 0% of each run, Pallas kernels for 51% -> 0%
where the time goes in v3:
time: 127 us; the launch traced here: 125 us
  Pallas kernels  119 us (94%)
  local copies, waits for them, and re-layouts  3.38 us (3%)
  other arithmetic  2.88 us (2%)
    pallas_call x1, Pallas kernels, layer(): pl.pallas_call(layer_kernel, out_shape=(shape((2, OCT, 16, 128), BF), sha...  115 us
    pallas_call x1, Pallas kernels, finish(): pl.pallas_call(finish_kernel, out_shape=jax.ShapeDtypeStruct((4, NLON, 12...  3.39 us
    unnamed x6, local copies, waits for them, and re-layouts  3.38 us
    reduce_sum x1, other arithmetic, per_device(): squares = jnp.sum(x * x, axis=-1)  2.88 us

profile of v3, /device:TPU:1, one launch (start us, length us, event | category | flops | bytes accessed | tf_op | source)
XLA Modules:
  0.0 125.1 jit_solution(8338029348274962590)
XLA Ops:
  0.0 2.9 %multiply_reduce_fusion.sq_ref = f32[4,1440]{1,0:T(4,128)} fusion(bf16[4,1440,128]{2,1,0:T(8,128)(2,1)} %f_ref.1), kind=kLoop, calls=%fused_computation | loop fusion | flops 2206080 | bytes 1497600 | tf_op jit(solution)/shard_map/reduce_sum | solution.py:497
  2.9 115.4 %layer.1 = (bf16[2,180,16,128]{3,2,1,0:T(8,128)(2,1)}, bf16[64,16,128]{2,1,0:T(8,128)(2,1)}, bf16[192,1440]{1,0:T(8,128)(2,1)}) custom-call(bf16[4,1440,128]{2,1,0:T(8,128)(2,1)} %f_ref.1, f32[4,1440]{1,0:T(4,128)} %multiply_reduce_fusion.sq_ref, bf16[1,128]{1,0:T(2,128)(2,1)} %bitcast.5, bf16[3,512,128]{2,1,0:T(8,128)(2,1)} %bitcast.3, ...), custom_call_target="tpu_custom_call" | custom-call | tf_op jit(solution)/shard_map/layer/pallas_call | solution.py:436
  118.3 0.0 copy-start
  118.3 1.4 %copy-done = bf16[2,180,16,128]{3,2,1,0:T(8,128)(2,1)S(1)} copy-done((bf16[2,180,16,128]{3,2,1,0:T(8,128)(2,1)S(1)}, bf16[2,180,16,128]{3,2,1,0:T(8,128)(2,1)}, u32[]{:S(2)}) %copy-start) | copy-done | bytes 1474584
  119.7 0.0 copy-start.1
  119.7 1.1 copy-done.1
  120.8 0.0 copy-start.2
  120.8 0.9 copy-done.2
  121.7 3.4 %finish.1 = bf16[4,1440,128]{2,1,0:T(8,128)(2,1)} custom-call(bf16[2,180,16,128]{3,2,1,0:T(8,128)(2,1)S(1)} %copy-done, bf16[192,1440]{1,0:T(8,128)(2,1)S(1)} %copy-done.1, bf16[64,16,128]{2,1,0:T(8,128)(2,1)S(1)} %copy-done.2), custom_call_target="tpu_custom_call" | custom-call | tf_op jit(solution)/shard_map/finish/pallas_call | solution.py:485
Async XLA Ops:
  118.3 1.4 %copy-start = (bf16[2,180,16,128]{3,2,1,0:T(8,128)(2,1)S(1)}, bf16[2,180,16,128]{3,2,1,0:T(8,128)(2,1)}, u32[]{:S(2)}) copy-start(bf16[2,180,16,128]{3,2,1,0:T(8,128)(2,1)} %get-tuple-element.8.local_ref) | copy-start | bytes 4423684
  119.7 1.1 copy-start.1
  120.8 0.9 copy-start.2

commit v4 on v3

--- a/solution.py
+++ b/solution.py
@@ -21,7 +21,6 @@
 BF = jnp.bfloat16
 DMA = pltpu.SemaphoreType.DMA
 VMEM = pl.BlockSpec(memory_space=pltpu.VMEM)
-ANY = pl.BlockSpec(memory_space=pl.ANY)
 TN = (((0,), (0,)), ((), ()))
 NT = (((1,), (1,)), ((), ()))
 
@@ -132,17 +131,18 @@
 
 
 def layer_kernel(
-    f_ref, sq_ref, gain_ref, wq_ref, wo_ref, bias_ref, reach_ref, mg_ref, ws_ref,
-    out_ref, modes_ref, t_ref,
+    f_ref, gain_ref, wq_ref, wo_ref, bias_ref, reach_ref, mg_ref, ws_ref,
+    out_ref,
     x_s, win_s, w_s, meta_s, metas_s, stat_s, tab_s, leg_s, e_s, send1_s, got_s, g_s, send2_s,
-    q_s, k_s, v_s, b_s, t_s, a_s, s_s, p_s, l_s, r_s, y_s,
-    lsem, statsem, metasem, w1sem, wbsem, w2sem, ssem, usem, nsem, hsem, a1sem, a2sem, gsem, bsem,
+    q_s, k_s, v_s, b_s, t_s, a_s, s_s, p_s, l_s, r_s, y_s, got2_s, local_s, t16_s, wave_s,
+    lsem, statsem, metasem, w1sem, wxsem, wbsem, w2sem, ssem, usem, nsem, hsem, a1sem, a2sem, gsem, bsem,
 ):
     lat, ch, group, zlo = place()
     me = zlo * 4 + ch
     has_next = group < 15
     has_prev = group > 0
     quarter = pl.ds(pl.multiple_of((group // 4) * 128, 128), 128)
+    sixteenth = pl.ds(pl.multiple_of(group * 32, 32), 32)
     sib = ch + 1 - 2 * (ch % 2)
     across = (ch + 2) % 4
     loop(1, 64, lambda d: signal(((lat + d) % 64, ch)))
@@ -152,7 +152,14 @@
     for d in range(1, 4):
         signal(((lat + 16 * d) % 64, sib))
 
-    stat_s[ch] = sq_ref[...]
+    ones = jnp.ones((8, 256), BF)
+    for r in range(4):
+        x = f_ref[r].astype(F32)
+        x = x * x
+        high = x.astype(BF)
+        both = jnp.concatenate([high, (x - high.astype(F32)).astype(BF)], axis=1)
+        sums = lax.dot_general(ones, both, NT, preferred_element_type=F32)
+        stat_s[ch, r : r + 1, :] = sums[0:1]
     gain = gain_ref[...].astype(F32)
     meta_s[...] = jnp.zeros_like(meta_s)
     for a in range(5):
@@ -180,12 +187,12 @@
     pl.semaphore_wait(pltpu.get_barrier_semaphore(), 78)
 
     for d in range(1, 4):
-        remote(sq_ref, stat_s.at[ch], statsem.at[0], statsem.at[1], (lat, (ch + d) % 4))
+        remote(stat_s.at[ch], stat_s.at[ch], statsem.at[0], statsem.at[1], (lat, (ch + d) % 4))
     for d in range(1, 4):
         remote(meta_s, metas_s.at[me], metasem.at[0], metasem.at[1], (lat, (ch + d) % 4))
         remote(meta_s, metas_s.at[me], metasem.at[0], metasem.at[1], (group * 4 + (zlo + d) % 4, ch))
-    remote(wq_ref.at[:, quarter], w_s.at[pl.ds(ch * 4, 3), quarter], w1sem.at[0], w1sem.at[1], (lat, across))
-    remote(wo_ref.at[quarter], w_s.at[ch * 4 + 3, quarter], w1sem.at[0], w1sem.at[1], (lat, across))
+    remote(wq_ref.at[:, sixteenth], w_s.at[pl.ds(ch * 4, 3), sixteenth], w1sem.at[0], w1sem.at[1], (lat, across))
+    remote(wo_ref.at[sixteenth], w_s.at[ch * 4 + 3, sixteenth], w1sem.at[0], w1sem.at[1], (lat, across))
     remote(wq_ref, w_s.at[pl.ds(ch * 4, 3)], wbsem.at[0], wbsem.at[1], (lat, sib))
     remote(wo_ref, w_s.at[ch * 4 + 3], wbsem.at[0], wbsem.at[1], (lat, sib))
     own = [
@@ -214,18 +221,34 @@
         def _():
             start(x_s.at[src, pl.ds(s - 1, 14)], win_s.at[dst, ch], 0)
 
-    def spread(pair, ss, rs):
-        def one(d):
-            w = (me + d) % 16
-            move(w, pair, 1, 1 + 2 * zlo + pair, lambda a, b, n: remote(a, b, ss, rs, ring_dev(w, group)))
-
-        loop(1, 16, one)
+    def to(pair, ss, rs, dz, dc):
+        z = ((ch // 2) * 4 + zlo + dz) % 8
+        w = (z % 4) * 4 + (z // 4) * 2 + (ch + dc) % 2
+        move(w, pair, 1, 1 + 2 * zlo + pair, lambda a, b, n: remote(a, b, ss, rs, ring_dev(w, group)))
+
+    def near(pair, ss, rs):
+        def one(t):
+            u = t // 2
+            dz = jnp.where(u == 4, 0, jnp.where(u % 2 == 0, u // 2 + 1, 7 - u // 2))
+            to(pair, ss, rs, dz, jnp.where(t == 8, 1, t % 2))
+
+        loop(0, 9, one)
+
+    def far(pair, ss, rs):
+        def one(t):
+            u = t // 2
+            to(pair, ss, rs, jnp.where(u == 0, 3, jnp.where(u == 1, 5, 4)), t % 2)
+
+        loop(0, 6, one)
 
     move(me, 0, 2, 1 + 2 * zlo, lambda a, b, n: pltpu.make_async_copy(a, b, lsem.at[n]).start())
     urgent = jnp.where(zlo == 3, 1, 0)
-    spread(urgent, ssem.at[0], usem.at[jnp.where(zlo == 0, 1, jnp.where(zlo == 3, 2, 0))])
-
-    tables(tab_s, t_ref)
+    first = (urgent, ssem.at[0], usem.at[jnp.where(zlo == 0, 1, jnp.where(zlo == 3, 2, 0))])
+    second = (1 - urgent, ssem.at[1], nsem)
+    near(*first)
+    far(*first)
+
+    tables(tab_s, t16_s)
     wait_bytes(stat_s.at[pl.ds(0, 3)], statsem.at[1])
     scale = lax.rsqrt((stat_s[0] + stat_s[1] + stat_s[2] + stat_s[3]) * (1.0 / 512.0) + EPS)
     theta = ((lat * 4 + lax.broadcasted_iota(jnp.int32, (4, 128), 0)).astype(F32) + 0.5) * (math.pi / NLAT)
@@ -240,16 +263,40 @@
     loop(1, 64, lambda d: remote(send1_s.at[(lat + d) % 64], got_s.at[lat], a1sem.at[0], a1sem.at[1], ((lat + d) % 64, ch)))
     got_s[lat] = send1_s[lat]
 
-    spread(1 - urgent, ssem.at[1], nsem)
-
+    near(*second)
+
+    wait_bytes(w_s.at[pl.ds(across * 4, 4), sixteenth], w1sem.at[1])
+    strip = w_s.at[pl.ds(across * 4, 4), sixteenth]
+    for d in range(1, 4):
+        remote(strip, strip, wxsem.at[0], wxsem.at[1], (lat - group % 4 * 4 + (group + d) % 4 * 4, ch))
+    legendre(lat, leg_s, e_s)
     part = w_s.at[pl.ds(across * 4, 4), quarter]
-    wait_bytes(part, w1sem.at[1])
+    wait_bytes(w_s.at[pl.ds(0, 3), pl.ds(0, 128)], wxsem.at[1])
     remote(part, part, w2sem.at[0], w2sem.at[1], (lat, sib))
     for d in range(1, 4):
         remote(part, part, w2sem.at[0], w2sem.at[1], ((lat + 16 * d) % 64, ch))
         remote(part, part, w2sem.at[0], w2sem.at[1], ((lat + 16 * d) % 64, sib))
 
-    legendre(lat, leg_s, e_s)
+    @pl.when((me == 0) | (me == 15))
+    def _():
+        wait_bytes(win_s.at[pl.ds(0, 2), 0, pl.ds(0, 13)], lsem.at[0])
+        wait_bytes(win_s.at[pl.ds(0, 2), 0, pl.ds(0, 1)], lsem.at[1])
+
+    @pl.when((me != 0) & (me != 15))
+    def _():
+        wait_bytes(win_s.at[pl.ds(0, 2), 0], lsem.at[0])
+
+    def arrived(own_here, full, sem):
+        pl.when(own_here)(lambda: wait_bytes(win_s.at[pl.ds(0, full - 1), 0], sem))
+        pl.when(jnp.logical_not(own_here))(lambda: wait_bytes(win_s.at[pl.ds(0, full), 0], sem))
+
+    arrived(zlo == 0, 4, usem.at[1])
+    arrived(zlo == 3, 4, usem.at[2])
+    pl.when(has_next)(lambda: remote(win_s.at[8], win_s.at[0], hsem.at[0], hsem.at[1], ((lat + 4) % 64, ch)))
+    pl.when(has_prev)(lambda: remote(win_s.at[1], win_s.at[9], hsem.at[2], hsem.at[3], ((lat + 60) % 64, ch)))
+
+    far(*second)
+
 
     for copy in own:
         copy.wait()
@@ -275,31 +322,6 @@
     for z in range(4):
         r_s[z * 8 : z * 8 + 8, :] = jnp.dot(metas_s[z * 4 + ch, 16:24, :], pick, preferred_element_type=F32)
 
-    @pl.when((me == 0) | (me == 15))
-    def _():
-        wait_bytes(win_s.at[pl.ds(0, 2), 0, pl.ds(0, 13)], lsem.at[0])
-        wait_bytes(win_s.at[pl.ds(0, 2), 0, pl.ds(0, 1)], lsem.at[1])
-
-    @pl.when((me != 0) & (me != 15))
-    def _():
-        wait_bytes(win_s.at[pl.ds(0, 2), 0], lsem.at[0])
-
-    def arrived(own_here, full, sem):
-        pl.when(own_here)(lambda: wait_bytes(win_s.at[pl.ds(0, full - 1), 0], sem))
-        pl.when(jnp.logical_not(own_here))(lambda: wait_bytes(win_s.at[pl.ds(0, full), 0], sem))
-
-    arrived(zlo == 0, 4, usem.at[1])
-    arrived(zlo == 3, 4, usem.at[2])
-    pl.when(has_next)(lambda: remote(win_s.at[8], win_s.at[0], hsem.at[0], hsem.at[1], ((lat + 4) % 64, ch)))
-    pl.when(has_prev)(lambda: remote(win_s.at[1], win_s.at[9], hsem.at[2], hsem.at[3], ((lat + 60) % 64, ch)))
-
-    wait_bytes(got_s.at[pl.ds(0, 63)], a1sem.at[1])
-    coef = jnp.dot(e_s[...], got_s[...].reshape(1024, 128), preferred_element_type=F32)
-    coef = coef.reshape(3, DEG, 128) * mg_ref[...][None]
-    g_s[ch] = coef.reshape(3 * DEG, 128).astype(BF)
-    for d in range(1, 4):
-        remote(g_s.at[ch], g_s.at[ch], gsem.at[0], gsem.at[1], (lat, (ch + d) % 4))
-
     def weights(t):
         return jnp.concatenate([w_s[k * 4 + t] for k in range(4)], axis=1)
 
@@ -326,19 +348,6 @@
     wait_bytes(w_s.at[pl.ds(0, 7)], w2sem.at[1])
     arrived((zlo == 1) | (zlo == 2), 8, usem.at[0])
     loop(0, 4, lambda i: project(1 + 2 * i + i // 3, True))
-
-    wait_bytes(g_s.at[pl.ds(0, 3)], gsem.at[1])
-    gained = jnp.concatenate([g_s[k] for k in range(4)], axis=1)
-    mixed = jnp.dot(gained, ws_ref[...].astype(BF), preferred_element_type=F32)
-    parts = []
-    for k in range(3):
-        twice = jnp.where((lat + 64 * k) % DEG == 0, 1.0, 2.0).astype(F32)
-        parts.append((mixed[k * DEG : k * DEG + DEG] * twice).astype(BF))
-    rows_out = lax.dot_general(e_s[...], jnp.concatenate(parts, axis=0), TN, preferred_element_type=F32)
-    send2_s[...] = rows_out.astype(BF).reshape(64, 16, 128)
-    loop(1, 64, lambda d: remote(send2_s.at[(lat + d) % 64], modes_ref.at[lat], a2sem.at[0], a2sem.at[1], ((lat + d) % 64, ch)))
-    acopy = pltpu.make_async_copy(send2_s.at[lat], modes_ref.at[lat], lsem.at[5])
-    acopy.start()
 
     wait_bytes(win_s.at[pl.ds(0, 5), pl.ds(0, 3)], nsem)
     loop(0, 4, lambda i: project(2 + 2 * i - i // 3, True))
@@ -375,22 +384,21 @@
             cols = slice(hp * 128, hp * 128 + 128)
             vb = v_s[pl.ds(i, 5), j * 32 : j * 32 + KB, cols].reshape(KEYS, 128)
             o = jnp.dot(p_s[n], vb, preferred_element_type=F32) / l_s[n]
-            a_s[i % 4, j * 32 : j * 32 + 32, cols] = jnp.where(left, o[:32], o[32:]).astype(BF)
+            a_s[i % 2, j * 32 : j * 32 + 32, cols] = jnp.where(left, o[:32], o[32:]).astype(BF)
 
     s = win_start(me)
     wide = win_start(me + 1) - s == 12
 
     def rows_of(step):
-        rg = (zlo + step) % 4
-        loop(0, 4, lambda r: attend_row(rg * 4 + r))
-        out = jnp.dot(a_s[...].reshape(384, 512), weights(3), preferred_element_type=F32).reshape(2, 2, 12, 8, 512)
+        pair = (2 * zlo + step) % 8
+        loop(0, 2, lambda r: attend_row(pair * 2 + r))
+        out = jnp.dot(a_s[...].reshape(192, 512), weights(3), preferred_element_type=F32).reshape(2, 12, 8, 512)
         for k in range(4):
-            for a in range(2):
-                both = jnp.stack([out[a, b, :, :, k * 128 : k * 128 + 128] for b in range(2)], axis=1)
-                y_s[rg * 2 + a, k] = both.reshape(12, 16, 128).astype(BF)
+            both = jnp.stack([out[b, :, :, k * 128 : k * 128 + 128] for b in range(2)], axis=1)
+            y_s[pair, k] = both.reshape(12, 16, 128).astype(BF)
 
         def give(k, n, start):
-            start(y_s.at[pl.ds(rg * 2, 2), k, pl.ds(0, n)], out_ref.at[:, pl.ds(s, n)])
+            start(y_s.at[pair, k, pl.ds(0, n)], local_s.at[pair % 2, pl.ds(s, n)])
 
         def both(k, start):
             pl.when(wide)(lambda: give(k, 12, start))
@@ -398,17 +406,46 @@
 
         for d in range(1, 4):
             k = (ch + d) % 4
-            both(k, lambda a, b, k=k: remote(a, b, bsem.at[0], bsem.at[1], (group * 4 + rg, k)))
-        pl.when(step == 0)(lambda: both(ch, lambda a, b: pltpu.make_async_copy(a, b, lsem.at[6]).start()))
-        pl.when(step > 0)(
-            lambda: both(ch, lambda a, b: remote(a, b, bsem.at[0], bsem.at[1], (group * 4 + rg, ch)))
-        )
-
-    loop(0, 4, rows_of)
+            both(k, lambda a, b, k=k: remote(a, b, bsem.at[0], bsem.at[1], (group * 4 + pair // 2, k)))
+        if isinstance(step, int):
+            both(ch, lambda a, b: pltpu.make_async_copy(a, b, lsem.at[5 + step]).start())
+        else:
+            both(ch, lambda a, b: remote(a, b, bsem.at[0], bsem.at[1], (group * 4 + pair // 2, ch)))
+
+    wait_bytes(got_s.at[pl.ds(0, 63)], a1sem.at[1])
+    coef = jnp.dot(e_s[...], got_s[...].reshape(1024, 128), preferred_element_type=F32)
+    coef = coef.reshape(3, DEG, 128) * mg_ref[...][None]
+    g_s[ch] = coef.reshape(3 * DEG, 128).astype(BF)
+    remote(g_s.at[ch], g_s.at[ch], gsem.at[0], gsem.at[1], (lat, across))
+    remote(g_s.at[ch], g_s.at[ch], gsem.at[2], gsem.at[3], (lat, sib))
+
+    rows_of(0)
+    wait_bytes(g_s.at[0], gsem.at[1])
+    remote(g_s.at[across], g_s.at[across], gsem.at[2], gsem.at[3], (lat, sib))
+    rows_of(1)
+    wait_bytes(g_s.at[pl.ds(0, 2)], gsem.at[3])
+    gained = jnp.concatenate([g_s[k] for k in range(4)], axis=1)
+    mixed = jnp.dot(gained, ws_ref[...].astype(BF), preferred_element_type=F32)
+    parts = []
+    for k in range(3):
+        twice = jnp.where((lat + 64 * k) % DEG == 0, 1.0, 2.0).astype(F32)
+        parts.append((mixed[k * DEG : k * DEG + DEG] * twice).astype(BF))
+    rows_out = lax.dot_general(e_s[...], jnp.concatenate(parts, axis=0), TN, preferred_element_type=F32)
+    send2_s[...] = rows_out.astype(BF).reshape(64, 16, 128)
+    loop(1, 64, lambda d: remote(send2_s.at[(lat + d) % 64], got2_s.at[lat], a2sem.at[0], a2sem.at[1], ((lat + d) % 64, ch)))
+    got2_s[lat] = send2_s[lat]
+
+    loop(2, 8, rows_of)
+
+    wait_bytes(got2_s.at[pl.ds(0, 63)], a2sem.at[1])
+    modes = lax.dot_general(sort_rows(), got2_s[...].reshape(1024, 128), TN, preferred_element_type=F32).astype(BF)
+    for r in range(4):
+        wave_s[r] = lax.dot_general(t16_s[...], modes[r * 192 : r * 192 + 192], TN, preferred_element_type=F32)
 
     wait_bytes(stat_s.at[pl.ds(0, 3)], statsem.at[0])
     wait_bytes(metas_s.at[pl.ds(0, 6)], metasem.at[0])
-    wait_bytes(part, w1sem.at[0])
+    wait_bytes(strip, w1sem.at[0])
+    wait_bytes(w_s.at[pl.ds(0, 3), pl.ds(0, 128)], wxsem.at[0])
     wait_bytes(w_s.at[pl.ds(0, 4)], wbsem.at[0])
     wait_bytes(w_s.at[pl.ds(0, 7)], w2sem.at[0])
     wait_bytes(win_s.at[pl.ds(0, 5), pl.ds(0, 3)], ssem.at[0])
@@ -416,18 +453,27 @@
     pl.when(has_next)(lambda: wait_bytes(win_s.at[0], hsem.at[0]))
     pl.when(has_prev)(lambda: wait_bytes(win_s.at[0], hsem.at[2]))
     wait_bytes(got_s.at[pl.ds(0, 63)], a1sem.at[0])
-    wait_bytes(g_s.at[pl.ds(0, 3)], gsem.at[0])
-    acopy.wait()
-    wait_bytes(modes_ref.at[pl.ds(0, 63)], a2sem.at[0])
-    wait_bytes(modes_ref.at[pl.ds(0, 63)], a2sem.at[1])
+    wait_bytes(g_s.at[0], gsem.at[0])
+    wait_bytes(g_s.at[pl.ds(0, 2)], gsem.at[2])
+    wait_bytes(got2_s.at[pl.ds(0, 63)], a2sem.at[0])
 
     def last(n):
-        wait_bytes(out_ref.at[:, pl.ds(0, n)], lsem.at[6])
-        wait_bytes(out_ref.at[:, pl.ds(0, 15 * n)], bsem.at[0])
-        wait_bytes(out_ref.at[:, pl.ds(0, OCT - n)], bsem.at[1])
+        wait_bytes(local_s.at[0, pl.ds(0, n)], lsem.at[5])
+        wait_bytes(local_s.at[0, pl.ds(0, n)], lsem.at[6])
+        wait_bytes(local_s.at[:, pl.ds(0, 15 * n)], bsem.at[0])
+        wait_bytes(local_s.at[:, pl.ds(0, OCT - n)], bsem.at[1])
 
     pl.when(wide)(lambda: last(12))
     pl.when(jnp.logical_not(wide))(lambda: last(11))
+
+    def total(c):
+        lon = pl.ds(pl.multiple_of(c * 144, 16), 144)
+        for a in range(2):
+            part = local_s[a, pl.ds(c * 18, 18)].astype(F32).reshape(18, 2, 8, 128)
+            for b in range(2):
+                out_ref[2 * a + b, lon, :] = (wave_s[2 * a + b, lon, :] + part[:, b].reshape(144, 128)).astype(BF)
+
+    loop(0, 10, total)
 
 
 def layer(*args):
@@ -435,9 +481,9 @@
     vm = pltpu.VMEM
     return pl.pallas_call(
         layer_kernel,
-        out_shape=(shape((2, OCT, 16, 128), BF), shape((64, 16, 128), BF), shape((2 * DEG, NLON), BF)),
-        in_specs=[VMEM] * 9,
-        out_specs=[ANY, ANY, VMEM],
+        out_shape=shape((4, NLON, 128), BF),
+        in_specs=[VMEM] * 8,
+        out_specs=VMEM,
         scratch_shapes=[
             vm((2, OCT, 16, 128), BF),
             vm((10, 4, 14, 16, 128), BF),
@@ -457,14 +503,18 @@
             vm((20, 112, 512), BF),
             vm((4, 64, KEYS), F32),
             vm((4, 64, KEYS), F32),
-            vm((4, 96, 512), BF),
+            vm((2, 96, 512), BF),
             vm((12, 64, KEYS), F32),
             vm((12, 64, KEYS), BF),
             vm((12, 64, 128), F32),
             vm((32, KEYS), F32),
             vm((8, 4, 12, 16, 128), BF),
-            DMA((7,)), DMA((2,)), DMA((2,)), DMA((2,)), DMA((2,)), DMA((2,)), DMA((2,)), DMA((3,)), DMA,
-            DMA((4,)), DMA((2,)), DMA((2,)), DMA((2,)), DMA((2,)),
+            vm((64, 16, 128), BF),
+            vm((2, OCT, 16, 128), BF),
+            vm((2 * DEG, NLON), BF),
+            vm((4, NLON, 128), F32),
+            DMA((7,)), DMA((2,)), DMA((2,)), DMA((2,)), DMA((2,)), DMA((2,)), DMA((2,)), DMA((2,)), DMA((3,)), DMA,
+            DMA((4,)), DMA((2,)), DMA((2,)), DMA((4,)), DMA((2,)),
         ],
         compiler_params=pltpu.CompilerParams(
             collective_id=0, has_side_effects=True, vmem_limit_bytes=56 * 1024 * 1024
@@ -473,31 +523,9 @@
     )(*args)
 
 
-def finish_kernel(local_ref, t_ref, got_ref, out_ref):
-    modes = lax.dot_general(sort_rows(), got_ref[...].reshape(1024, 128), TN, preferred_element_type=F32).astype(BF)
-    for r in range(4):
-        wave = lax.dot_general(t_ref[...], modes[r * 192 : r * 192 + 192], TN, preferred_element_type=F32)
-        local = local_ref[r // 2].astype(F32).reshape(OCT, 2, 8, 128)[:, r % 2].reshape(NLON, 128)
-        out_ref[r] = (wave + local).astype(BF)
-
-
-def finish(*args):
-    return pl.pallas_call(
-        finish_kernel,
-        out_shape=jax.ShapeDtypeStruct((4, NLON, 128), BF),
-        in_specs=[VMEM] * 3,
-        out_specs=VMEM,
-        compiler_params=pltpu.CompilerParams(vmem_limit_bytes=40 * 1024 * 1024),
-        name="finish",
-    )(*args)
-
-
 def per_device(fields, norm_gain, w_qkv, w_out, rel_bias, stencil_reach, mode_gain, w_spec):
-    x = fields.astype(F32)
-    squares = jnp.sum(x * x, axis=-1)
-    local, modes, table = layer(
+    return layer(
         fields,
-        squares,
         norm_gain.reshape(1, 128),
         jnp.transpose(w_qkv, (1, 0, 2)),
         w_out,
@@ -506,7 +534,6 @@
         mode_gain,
         w_spec,
     )
-    return finish(local, table, modes)
 
 
 def solution(mesh):

time: 127 us -> 114 us (0.90); the launches traced: 125 us -> 114 us
  Pallas kernels: 119 us -> 112 us
  other arithmetic: 2.88 us -> 0 us
    pallas_call x2 -> x1, Pallas kernels: 119 us -> 112 us  [layer(): pl.pallas_call(layer_kernel, out_shape=shape((4, NLON, 128), BF), in_spec...]
    reduce_sum x1 -> x0, other arithmetic: 2.88 us -> none  [per_device(): squares = jnp.sum(x * x, axis=-1)]
    unnamed x6 -> x1, local copies, waits for them, and re-layouts: 3.38 us -> 2.58 us
where the time goes in v4:
time: 114 us
  Pallas kernels  112 us (98%)
  local copies, waits for them, and re-layouts  2.58 us (2%)
    pallas_call x1, Pallas kernels, layer(): pl.pallas_call(layer_kernel, out_shape=shape((4, NLON, 128), BF), in_spec...  112 us
    unnamed x1, local copies, waits for them, and re-layouts  2.58 us

profile of v4, /device:TPU:1, one launch (start us, length us, event | category | flops | bytes accessed | tf_op | source)
XLA Modules:
  0.0 114.4 jit_solution(15618083535228587624)
XLA Ops:
  0.0 111.8 %layer.1 = bf16[4,1440,128]{2,1,0:T(8,128)(2,1)} custom-call(bf16[4,1440,128]{2,1,0:T(8,128)(2,1)} %f_ref.1, bf16[1,128]{1,0:T(2,128)(2,1)} %bitcast.5, bf16[3,512,128]{2,1,0:T(8,128)(2,1)} %bitcast.3, bf16[512,128]{1,0:T(8,128)(2,1)} %wo_ref.1, f32[5,2,17]{2,1,0:T(2,128)} %bitcast.4, s32[4,5]{1,0:T(4,128)} %reach_ref.1, f32[96,128]{1,0:T(8,128)} %mg_ref.1, ...), custom_call_target="tpu_custom_call" | custom-call | tf_op jit(solution)/shard_map/layer/pallas_call | solution.py:482
  111.8 2.6 %copy.10 = bf16[4,1440,128]{2,1,0:T(8,128)(2,1)} copy(bf16[4,1440,128]{2,1,0:T(8,128)(2,1)} %layer.1) | data formatting | bytes 2949120

commit v5 on v4

--- a/solution.py
+++ b/solution.py
@@ -350,11 +350,9 @@
     loop(0, 4, lambda i: project(1 + 2 * i + i // 3, True))
 
     wait_bytes(win_s.at[pl.ds(0, 5), pl.ds(0, 3)], nsem)
-    loop(0, 4, lambda i: project(2 + 2 * i - i // 3, True))
     pl.when(has_prev)(lambda: wait_bytes(win_s.at[0], hsem.at[1]))
-    project(0, False)
     pl.when(has_next)(lambda: wait_bytes(win_s.at[0], hsem.at[3]))
-    project(9, False)
+    loop(0, 2, lambda i: project(2 * zlo + i * jnp.where(zlo == 3, 1, 2), True))
 
     left = lax.broadcasted_iota(jnp.int32, (32, 128), 1) < 64
     blocks = [(j, hp) for j in range(3) for hp in range(4)]
@@ -420,9 +418,12 @@
     remote(g_s.at[ch], g_s.at[ch], gsem.at[2], gsem.at[3], (lat, sib))
 
     rows_of(0)
+    loop(0, 3, lambda i: project(jnp.where(i < zlo, 2 * i, jnp.where(i == 2, 7, 4 + 2 * i)), True))
+    project(9, False)
+    rows_of(1)
     wait_bytes(g_s.at[0], gsem.at[1])
     remote(g_s.at[across], g_s.at[across], gsem.at[2], gsem.at[3], (lat, sib))
-    rows_of(1)
+    loop(2, 5, rows_of)
     wait_bytes(g_s.at[pl.ds(0, 2)], gsem.at[3])
     gained = jnp.concatenate([g_s[k] for k in range(4)], axis=1)
     mixed = jnp.dot(gained, ws_ref[...].astype(BF), preferred_element_type=F32)
@@ -435,7 +436,7 @@
     loop(1, 64, lambda d: remote(send2_s.at[(lat + d) % 64], got2_s.at[lat], a2sem.at[0], a2sem.at[1], ((lat + d) % 64, ch)))
     got2_s[lat] = send2_s[lat]
 
-    loop(2, 8, rows_of)
+    loop(5, 8, rows_of)
 
     wait_bytes(got2_s.at[pl.ds(0, 63)], a2sem.at[1])
     modes = lax.dot_general(sort_rows(), got2_s[...].reshape(1024, 128), TN, preferred_element_type=F32).astype(BF)

time: 114 us -> 112 us (0.982); the launches traced: 114 us -> 111 us
  Pallas kernels: 112 us -> 108 us
    pallas_call x1, Pallas kernels: 112 us -> 108 us  [layer(): pl.pallas_call(layer_kernel, out_shape=shape((4, NLON, 128), BF), in_spec...]
where the time goes in v5:
time: 112 us; the launch traced here: 111 us
  Pallas kernels  108 us (96%)
  local copies, waits for them, and re-layouts  2.58 us (2%)
    pallas_call x1, Pallas kernels, layer(): pl.pallas_call(layer_kernel, out_shape=shape((4, NLON, 128), BF), in_spec...  108 us
    unnamed x1, local copies, waits for them, and re-layouts  2.58 us

profile of v5, /device:TPU:1, one launch (start us, length us, event | category | flops | bytes accessed | tf_op | source)
XLA Modules:
  0.0 110.7 jit_solution(14279351160271611498)
XLA Ops:
  0.0 108.1 %layer.1 = bf16[4,1440,128]{2,1,0:T(8,128)(2,1)} custom-call(bf16[4,1440,128]{2,1,0:T(8,128)(2,1)} %f_ref.1, bf16[1,128]{1,0:T(2,128)(2,1)} %bitcast.5, bf16[3,512,128]{2,1,0:T(8,128)(2,1)} %bitcast.3, bf16[512,128]{1,0:T(8,128)(2,1)} %wo_ref.1, f32[5,2,17]{2,1,0:T(2,128)} %bitcast.4, s32[4,5]{1,0:T(4,128)} %reach_ref.1, f32[96,128]{1,0:T(8,128)} %mg_ref.1, ...), custom_call_target="tpu_custom_call" | custom-call | tf_op jit(solution)/shard_map/layer/pallas_call | solution.py:483
  108.1 2.6 %copy.10 = bf16[4,1440,128]{2,1,0:T(8,128)(2,1)} copy(bf16[4,1440,128]{2,1,0:T(8,128)(2,1)} %layer.1) | data formatting | bytes 2949120

commit v6 on v5

--- a/solution.py
+++ b/solution.py
@@ -135,7 +135,7 @@
     out_ref,
     x_s, win_s, w_s, meta_s, metas_s, stat_s, tab_s, leg_s, e_s, send1_s, got_s, g_s, send2_s,
     q_s, k_s, v_s, b_s, t_s, a_s, s_s, p_s, l_s, r_s, y_s, got2_s, local_s, t16_s, wave_s,
-    lsem, statsem, metasem, w1sem, wxsem, wbsem, w2sem, ssem, usem, nsem, hsem, a1sem, a2sem, gsem, bsem,
+    lsem, fsem, statsem, metasem, w1sem, wxsem, wbsem, w2sem, ssem, usem, nsem, hsem, a1sem, a2sem, gsem, bsem,
 ):
     lat, ch, group, zlo = place()
     me = zlo * 4 + ch
@@ -143,6 +143,7 @@
     has_prev = group > 0
     quarter = pl.ds(pl.multiple_of((group // 4) * 128, 128), 128)
     sixteenth = pl.ds(pl.multiple_of(group * 32, 32), 32)
+    wide = ch == 3
     sib = ch + 1 - 2 * (ch % 2)
     across = (ch + 2) % 4
     loop(1, 64, lambda d: signal(((lat + d) % 64, ch)))
@@ -172,9 +173,13 @@
         lon = pl.ds(pl.multiple_of(c * 144, 16), 144)
         for a in range(2):
             two = [f_ref[2 * a + b, lon, :].astype(F32).reshape(18, 8, 128) for b in range(2)]
-            x_s[a, pl.ds(c * 18, 18)] = jnp.stack(two, axis=1).reshape(18, 16, 128).astype(BF)
+            x_s[pl.ds(a * OCT + c * 18, 18)] = jnp.stack(two, axis=1).reshape(18, 16, 128).astype(BF)
 
     loop(0, 10, interleave)
+
+    @pl.when(jnp.logical_not(wide))
+    def _():
+        win_s[1:9, :, 13] = jnp.zeros_like(win_s[1:9, :, 13])
 
     @pl.when(jnp.logical_not(has_prev))
     def _():
@@ -203,28 +208,30 @@
     for copy in own:
         copy.start()
 
-    def move(w, src_pair, pairs, dst_pair, start):
+    def move(w, pair, start):
         s = win_start(w)
-        src, dst = pl.ds(src_pair, pairs), pl.ds(dst_pair, pairs)
-        edge = (w == 0) | (w == 15)
-
-        @pl.when(edge)
+        src, dst = pair * OCT, 1 + 2 * zlo + pair
+
+        def piece(at, n, to, sem):
+            start(x_s.at[pl.ds(src + at, n)], win_s.at[dst, ch, pl.ds(to, n)], sem)
+
+        @pl.when(w == 0)
         def _():
-            a_src = jnp.where(w == 0, 0, s - 1)
-            a_dst = jnp.where(w == 0, 1, 0)
-            b_src = jnp.where(w == 0, OCT - 1, 0)
-            b_dst = jnp.where(w == 0, 0, 13)
-            start(x_s.at[src, pl.ds(a_src, 13)], win_s.at[dst, ch, pl.ds(a_dst, 13)], 0)
-            start(x_s.at[src, pl.ds(b_src, 1)], win_s.at[dst, ch, pl.ds(b_dst, 1)], 1)
-
-        @pl.when(jnp.logical_not(edge))
+            piece(0, 12, 1, 0)
+            piece(OCT - 1, 1, 0, 1)
+
+        @pl.when(w == 15)
         def _():
-            start(x_s.at[src, pl.ds(s - 1, 14)], win_s.at[dst, ch], 0)
+            piece(s - 1, 13, 0, 0)
+            piece(0, 1, 13, 1)
+
+        pl.when((w % 4 == 3) & (w != 15))(lambda: piece(s - 1, 14, 0, 0))
+        pl.when((w % 4 != 3) & (w != 0))(lambda: piece(s - 1, 13, 0, 0))
 
     def to(pair, ss, rs, dz, dc):
         z = ((ch // 2) * 4 + zlo + dz) % 8
         w = (z % 4) * 4 + (z // 4) * 2 + (ch + dc) % 2
-        move(w, pair, 1, 1 + 2 * zlo + pair, lambda a, b, n: remote(a, b, ss, rs, ring_dev(w, group)))
+        move(w, pair, lambda a, b, n: remote(a, b, ss, rs, ring_dev(w, group)))
 
     def near(pair, ss, rs):
         def one(t):
@@ -241,7 +248,8 @@
 
         loop(0, 6, one)
 
-    move(me, 0, 2, 1 + 2 * zlo, lambda a, b, n: pltpu.make_async_copy(a, b, lsem.at[n]).start())
+    for pair in range(2):
+        move(me, pair, lambda a, b, n, pair=pair: pltpu.make_async_copy(a, b, fsem.at[pair * 2 + n]).start())
     urgent = jnp.where(zlo == 3, 1, 0)
     first = (urgent, ssem.at[0], usem.at[jnp.where(zlo == 0, 1, jnp.where(zlo == 3, 2, 0))])
     second = (1 - urgent, ssem.at[1], nsem)
@@ -277,18 +285,16 @@
         remote(part, part, w2sem.at[0], w2sem.at[1], ((lat + 16 * d) % 64, ch))
         remote(part, part, w2sem.at[0], w2sem.at[1], ((lat + 16 * d) % 64, sib))
 
-    @pl.when((me == 0) | (me == 15))
-    def _():
-        wait_bytes(win_s.at[pl.ds(0, 2), 0, pl.ds(0, 13)], lsem.at[0])
-        wait_bytes(win_s.at[pl.ds(0, 2), 0, pl.ds(0, 1)], lsem.at[1])
-
-    @pl.when((me != 0) & (me != 15))
-    def _():
-        wait_bytes(win_s.at[pl.ds(0, 2), 0], lsem.at[0])
+    for n in range(2):
+        move(me, n, lambda a, b, part, n=n: wait_bytes(b, fsem.at[n * 2 + part]))
 
     def arrived(own_here, full, sem):
-        pl.when(own_here)(lambda: wait_bytes(win_s.at[pl.ds(0, full - 1), 0], sem))
-        pl.when(jnp.logical_not(own_here))(lambda: wait_bytes(win_s.at[pl.ds(0, full), 0], sem))
+        for n in (full - 1, full):
+            this = own_here if n < full else jnp.logical_not(own_here)
+            pl.when(this & wide)(lambda n=n: wait_bytes(win_s.at[pl.ds(0, n), 0], sem))
+            pl.when(this & jnp.logical_not(wide))(
+                lambda n=n: wait_bytes(win_s.at[pl.ds(0, n), 0, pl.ds(0, 13)], sem)
+            )
 
     arrived(zlo == 0, 4, usem.at[1])
     arrived(zlo == 3, 4, usem.at[2])
@@ -349,7 +355,8 @@
     arrived((zlo == 1) | (zlo == 2), 8, usem.at[0])
     loop(0, 4, lambda i: project(1 + 2 * i + i // 3, True))
 
-    wait_bytes(win_s.at[pl.ds(0, 5), pl.ds(0, 3)], nsem)
+    pl.when(wide)(lambda: wait_bytes(win_s.at[pl.ds(0, 5), pl.ds(0, 3)], nsem))
+    pl.when(jnp.logical_not(wide))(lambda: wait_bytes(win_s.at[pl.ds(0, 5), pl.ds(0, 3), pl.ds(0, 13)], nsem))
     pl.when(has_prev)(lambda: wait_bytes(win_s.at[0], hsem.at[1]))
     pl.when(has_next)(lambda: wait_bytes(win_s.at[0], hsem.at[3]))
     loop(0, 2, lambda i: project(2 * zlo + i * jnp.where(zlo == 3, 1, 2), True))
@@ -385,7 +392,6 @@
             a_s[i % 2, j * 32 : j * 32 + 32, cols] = jnp.where(left, o[:32], o[32:]).astype(BF)
 
     s = win_start(me)
-    wide = win_start(me + 1) - s == 12
 
     def rows_of(step):
         pair = (2 * zlo + step) % 8
@@ -449,8 +455,9 @@
     wait_bytes(w_s.at[pl.ds(0, 3), pl.ds(0, 128)], wxsem.at[0])
     wait_bytes(w_s.at[pl.ds(0, 4)], wbsem.at[0])
     wait_bytes(w_s.at[pl.ds(0, 7)], w2sem.at[0])
-    wait_bytes(win_s.at[pl.ds(0, 5), pl.ds(0, 3)], ssem.at[0])
-    wait_bytes(win_s.at[pl.ds(0, 5), pl.ds(0, 3)], ssem.at[1])
+    for n in range(2):
+        pl.when(wide)(lambda n=n: wait_bytes(x_s.at[pl.ds(0, 198)], ssem.at[n]))
+        pl.when(jnp.logical_not(wide))(lambda n=n: wait_bytes(x_s.at[pl.ds(0, 199)], ssem.at[n]))
     pl.when(has_next)(lambda: wait_bytes(win_s.at[0], hsem.at[0]))
     pl.when(has_prev)(lambda: wait_bytes(win_s.at[0], hsem.at[2]))
     wait_bytes(got_s.at[pl.ds(0, 63)], a1sem.at[0])
@@ -486,7 +493,7 @@
         in_specs=[VMEM] * 8,
         out_specs=VMEM,
         scratch_shapes=[
-            vm((2, OCT, 16, 128), BF),
+            vm((2 * OCT, 16, 128), BF),
             vm((10, 4, 14, 16, 128), BF),
             vm((16, 512, 128), BF),
             vm((24, 128), F32),
@@ -514,7 +521,7 @@
             vm((2, OCT, 16, 128), BF),
             vm((2 * DEG, NLON), BF),
             vm((4, NLON, 128), F32),
-            DMA((7,)), DMA((2,)), DMA((2,)), DMA((2,)), DMA((2,)), DMA((2,)), DMA((2,)), DMA((2,)), DMA((3,)), DMA,
+            DMA((7,)), DMA((4,)), DMA((2,)), DMA((2,)), DMA((2,)), DMA((2,)), DMA((2,)), DMA((2,)), DMA((2,)), DMA((3,)), DMA,
             DMA((4,)), DMA((2,)), DMA((2,)), DMA((4,)), DMA((2,)),
         ],
         compiler_params=pltpu.CompilerParams(

time: 112 us -> 115 us (1.027)
  Pallas kernels: 108 us -> 112 us
    pallas_call x1, Pallas kernels: 108 us -> 112 us  [layer(): pl.pallas_call(layer_kernel, out_shape=shape((4, NLON, 128), BF), in_spec...]
where the time goes in v6:
time: 115 us
  Pallas kernels  112 us (97%)
  local copies, waits for them, and re-layouts  2.58 us (2%)
    pallas_call x1, Pallas kernels, layer(): pl.pallas_call(layer_kernel, out_shape=shape((4, NLON, 128), BF), in_spec...  112 us
    unnamed x1, local copies, waits for them, and re-layouts  2.58 us

profile of v6, /device:TPU:1, one launch (start us, length us, event | category | flops | bytes accessed | tf_op | source)
XLA Modules:
  0.0 114.6 jit_solution(3177534029425171386)
XLA Ops:
  0.0 112.0 %layer.1 = bf16[4,1440,128]{2,1,0:T(8,128)(2,1)} custom-call(bf16[4,1440,128]{2,1,0:T(8,128)(2,1)} %f_ref.1, bf16[1,128]{1,0:T(2,128)(2,1)} %bitcast.5, bf16[3,512,128]{2,1,0:T(8,128)(2,1)} %bitcast.3, bf16[512,128]{1,0:T(8,128)(2,1)} %wo_ref.1, f32[5,2,17]{2,1,0:T(2,128)} %bitcast.4, s32[4,5]{1,0:T(4,128)} %reach_ref.1, f32[96,128]{1,0:T(8,128)} %mg_ref.1, ...), custom_call_target="tpu_custom_call" | custom-call | tf_op jit(solution)/shard_map/layer/pallas_call | solution.py:490
  112.0 2.6 %copy.10 = bf16[4,1440,128]{2,1,0:T(8,128)(2,1)} copy(bf16[4,1440,128]{2,1,0:T(8,128)(2,1)} %layer.1) | data formatting | bytes 2949120

commit v7 on v5

--- a/solution.py
+++ b/solution.py
@@ -152,14 +152,6 @@
     for d in range(1, 4):
         signal(((lat + 16 * d) % 64, sib))
 
-    ones = jnp.ones((8, 256), BF)
-    for r in range(4):
-        x = f_ref[r].astype(F32)
-        x = x * x
-        high = x.astype(BF)
-        both = jnp.concatenate([high, (x - high.astype(F32)).astype(BF)], axis=1)
-        sums = lax.dot_general(ones, both, NT, preferred_element_type=F32)
-        stat_s[ch, r : r + 1, :] = sums[0:1]
     gain = gain_ref[...].astype(F32)
     meta_s[...] = jnp.zeros_like(meta_s)
     for a in range(5):
@@ -186,8 +178,6 @@
 
     pl.semaphore_wait(pltpu.get_barrier_semaphore(), 78)
 
-    for d in range(1, 4):
-        remote(stat_s.at[ch], stat_s.at[ch], statsem.at[0], statsem.at[1], (lat, (ch + d) % 4))
     for d in range(1, 4):
         remote(meta_s, metas_s.at[me], metasem.at[0], metasem.at[1], (lat, (ch + d) % 4))
         remote(meta_s, metas_s.at[me], metasem.at[0], metasem.at[1], (group * 4 + (zlo + d) % 4, ch))
@@ -246,6 +236,17 @@
     first = (urgent, ssem.at[0], usem.at[jnp.where(zlo == 0, 1, jnp.where(zlo == 3, 2, 0))])
     second = (1 - urgent, ssem.at[1], nsem)
     near(*first)
+
+    ones = jnp.ones((8, 256), BF)
+    for r in range(4):
+        x = f_ref[r].astype(F32)
+        x = x * x
+        high = x.astype(BF)
+        both = jnp.concatenate([high, (x - high.astype(F32)).astype(BF)], axis=1)
+        sums = lax.dot_general(ones, both, NT, preferred_element_type=F32)
+        stat_s[ch, r : r + 1, :] = sums[0:1]
+    for d in range(1, 4):
+        remote(stat_s.at[ch], stat_s.at[ch], statsem.at[0], statsem.at[1], (lat, (ch + d) % 4))
     far(*first)
 
     tables(tab_s, t16_s)

time: 112 us -> 112 us (level)
  no operation moved by 1% of the time
where the time goes in v7:
time: 112 us; the launch traced here: 111 us
  Pallas kernels  108 us (96%)
  local copies, waits for them, and re-layouts  2.58 us (2%)
    pallas_call x1, Pallas kernels, layer(): pl.pallas_call(layer_kernel, out_shape=shape((4, NLON, 128), BF), in_spec...  108 us
    unnamed x1, local copies, waits for them, and re-layouts  2.58 us

profile of v7, /device:TPU:1, one launch (start us, length us, event | category | flops | bytes accessed | tf_op | source)
XLA Modules:
  0.0 110.7 jit_solution(2685128508429907477)
XLA Ops:
  0.0 108.1 %layer.1 = bf16[4,1440,128]{2,1,0:T(8,128)(2,1)} custom-call(bf16[4,1440,128]{2,1,0:T(8,128)(2,1)} %f_ref.1, bf16[1,128]{1,0:T(2,128)(2,1)} %bitcast.5, bf16[3,512,128]{2,1,0:T(8,128)(2,1)} %bitcast.3, bf16[512,128]{1,0:T(8,128)(2,1)} %wo_ref.1, f32[5,2,17]{2,1,0:T(2,128)} %bitcast.4, s32[4,5]{1,0:T(4,128)} %reach_ref.1, f32[96,128]{1,0:T(8,128)} %mg_ref.1, ...), custom_call_target="tpu_custom_call" | custom-call | tf_op jit(solution)/shard_map/layer/pallas_call | solution.py:484
  108.1 2.6 %copy.10 = bf16[4,1440,128]{2,1,0:T(8,128)(2,1)} copy(bf16[4,1440,128]{2,1,0:T(8,128)(2,1)} %layer.1) | data formatting | bytes 2949120

commit v8 on v5

--- a/solution.py
+++ b/solution.py
@@ -410,6 +410,8 @@
         else:
             both(ch, lambda a, b: remote(a, b, bsem.at[0], bsem.at[1], (group * 4 + pair // 2, ch)))
 
+    rows_of(0)
+
     wait_bytes(got_s.at[pl.ds(0, 63)], a1sem.at[1])
     coef = jnp.dot(e_s[...], got_s[...].reshape(1024, 128), preferred_element_type=F32)
     coef = coef.reshape(3, DEG, 128) * mg_ref[...][None]
@@ -417,7 +419,6 @@
     remote(g_s.at[ch], g_s.at[ch], gsem.at[0], gsem.at[1], (lat, across))
     remote(g_s.at[ch], g_s.at[ch], gsem.at[2], gsem.at[3], (lat, sib))
 
-    rows_of(0)
     loop(0, 3, lambda i: project(jnp.where(i < zlo, 2 * i, jnp.where(i == 2, 7, 4 + 2 * i)), True))
     project(9, False)
     rows_of(1)

time: 112 us -> 114 us (1.018)
  Pallas kernels: 108 us -> 111 us
    pallas_call x1, Pallas kernels: 108 us -> 111 us  [layer(): pl.pallas_call(layer_kernel, out_shape=shape((4, NLON, 128), BF), in_spec...]
where the time goes in v8:
time: 114 us; the launch traced here: 113 us
  Pallas kernels  111 us (97%)
  local copies, waits for them, and re-layouts  2.58 us (2%)
    pallas_call x1, Pallas kernels, layer(): pl.pallas_call(layer_kernel, out_shape=shape((4, NLON, 128), BF), in_spec...  111 us
    unnamed x1, local copies, waits for them, and re-layouts  2.58 us

profile of v8, /device:TPU:1, one launch (start us, length us, event | category | flops | bytes accessed | tf_op | source)
XLA Modules:
  0.0 113.4 jit_solution(15407845467567596995)
XLA Ops:
  0.0 110.8 %layer.1 = bf16[4,1440,128]{2,1,0:T(8,128)(2,1)} custom-call(bf16[4,1440,128]{2,1,0:T(8,128)(2,1)} %f_ref.1, bf16[1,128]{1,0:T(2,128)(2,1)} %bitcast.5, bf16[3,512,128]{2,1,0:T(8,128)(2,1)} %bitcast.3, bf16[512,128]{1,0:T(8,128)(2,1)} %wo_ref.1, f32[5,2,17]{2,1,0:T(2,128)} %bitcast.4, s32[4,5]{1,0:T(4,128)} %reach_ref.1, f32[96,128]{1,0:T(8,128)} %mg_ref.1, ...), custom_call_target="tpu_custom_call" | custom-call | tf_op jit(solution)/shard_map/layer/pallas_call | solution.py:484
  110.8 2.6 %copy.10 = bf16[4,1440,128]{2,1,0:T(8,128)(2,1)} copy(bf16[4,1440,128]{2,1,0:T(8,128)(2,1)} %layer.1) | data formatting | bytes 2949120
